TPU v7x, 512 devices: a whole 4x8x8 slice. The times are simulated.
512 devices in a mesh: blk: 16 (over x, y_lo, core), site: 32 (over z, y_hi).
Axes of the slice: x: 4, y: 8 (y_hi: 4, y_lo: 2; y = y_hi * 2 + y_lo), z: 8, core: 2. Of those that a mesh axis runs over, the one named last changes fastest.
Arguments:
- modes: bfloat16 [2, 1, 256, 12, 4096], P(None, None, 'blk', None, 'site'), may hold values from -0.5 to 0.5
- momenta: int32 [4, 3], replicated, may hold values from -2 to 2
Outputs:
- meson_field: float32 [128, 256, 256], P('site', 'blk')
All inputs are finite; a program needn't handle non-finite values.
Results may differ from a plain program's by a relative error of at most 0.0027.
Values may be sent and summed in bfloat16 or wider, within the bound.
A program may use at most 128 MiB of HBM per device.

v0:
```python
import math

import jax
import jax.numpy as jnp
from jax import lax
from jax.sharding import PartitionSpec as P

LEXT = 48


TWO_PI = 2.0 * math.pi


def from_behind(shard, axis, by):
    devices = lax.axis_size(axis)
    return lax.ppermute(shard, axis, [(i, (i + by) % devices) for i in range(devices)])


def phase_table(momenta, first_site, site_count, extent):
    flat = first_site + jnp.arange(site_count, dtype=jnp.int32)
    coords = jnp.stack([flat % extent, flat // extent % extent, flat // (extent * extent)], 0)
    turns = jnp.mod(jnp.sum(momenta[:, :, None] * coords[None, :, :], axis=1), extent)
    angle = turns.astype(jnp.float32) * (TWO_PI / extent)
    return jnp.stack([jnp.cos(angle), jnp.sin(angle)], 1)


def apply_phase(fields, weights):
    scaled = (
        fields.astype(jnp.float32)[:, :, None, None]
        * weights[None, None, :, :, None, None, None, :]
    )
    return scaled.astype(jnp.bfloat16)


def rotate_left(phased):
    second = phased[:, :, :, 1]
    turned = jnp.stack([-second[1], second[0]], 0)
    return jnp.stack([phased[:, :, :, 0], turned], 3)


def extend(part):
    turned = jnp.stack([-part[1], part[0]], 0)
    return jnp.stack([part, turned], 0)


def conj_phased(phased):
    steps = phased.shape[1]
    grown = jnp.transpose(extend(phased), (2, 3, 4, 5, 6, 0, 1, 7, 8))
    return grown.reshape(steps, -1, 6 * phased.shape[-1])


def plain_side(fields):
    steps = fields.shape[1]
    return jnp.transpose(fields, (1, 2, 3, 0, 4, 5)).reshape(steps, -1, 6 * fields.shape[-1])


def batched_dot(first, second):
    return lax.dot_general(
        first, second, (((2,), (2,)), ((0,), (0,))), preferred_element_type=jnp.float32
    )


def split_terms(result):
    cosine_term = result[:, :, :, 0]
    sine_term = result[:, :, :, 1]
    column = jnp.arange(result.shape[-1], dtype=jnp.int32)
    signs = (1 - 2 * (column % 2)).astype(jnp.float32)
    return (cosine_term + sine_term, (cosine_term - sine_term) * signs)


def left_terms(left_own, moving, nmom):
    result = batched_dot(plain_side(moving), left_own)
    return split_terms(result.reshape(result.shape[0], result.shape[1], nmom, 2, -1))


def shards(modes, momenta):
    count = lax.axis_size("blk")
    half = count // 2
    here = lax.axis_index("blk")
    slots, steps, per_block, spin_colour, site_count = modes.shape
    nmom = momenta.shape[0]
    rows = steps * nmom * 32
    first_site = lax.axis_index("site") * site_count
    weights = phase_table(momenta, first_site, site_count, LEXT)
    fields = modes.reshape(slots, steps, per_block, 4, 3, site_count)
    left_own = conj_phased(rotate_left(apply_phase(fields, weights)))
    kept_list = []
    kept_slots = []
    pieces = []
    offsets = []
    kept_list.append(left_terms(left_own, fields, nmom)[0])
    kept_slots.append(0)
    moving = fields
    for dist in range(1, half + 1):
        moving = from_behind(moving, "blk", 1)
        kept, mirror = left_terms(left_own, moving, nmom)
        kept_list.append(kept)
        kept_slots.append(-dist % count)
        if dist < half:
            pieces.append(mirror)
            offsets.append(-dist)
    square = per_block * per_block
    kept_stack = jnp.stack(kept_list, 0).reshape(
        len(kept_list), steps, per_block, 4, nmom, per_block, 4, 2
    )
    kept_stack = jnp.transpose(kept_stack, (1, 4, 6, 3, 7, 0, 5, 2)).reshape(
        rows, len(kept_list), square
    )
    mirror_stack = jnp.stack(pieces, 0).reshape(
        len(pieces), steps, per_block, 4, nmom, per_block, 4, 2
    )
    mirror_stack = jnp.transpose(mirror_stack, (1, 4, 3, 6, 7, 0, 2, 5)).reshape(
        rows, len(pieces), square
    )
    kept_part, mirror_part = (
        lax.psum_scatter(kept_stack, "site", scatter_dimension=0, tiled=True),
        lax.psum_scatter(mirror_stack, "site", scatter_dimension=0, tiled=True),
    )
    share = kept_part.shape[0]
    empty = jnp.zeros((share, square), jnp.float32)
    placed = [empty] * count
    for index, slot in enumerate(kept_slots):
        placed[slot] = kept_part[:, index]
    for index, offset in enumerate(offsets):
        arrived = from_behind(mirror_part[:, index], "blk", offset)
        placed[-offset % count] = arrived
    whole = jnp.roll(jnp.stack(placed, 1), here, axis=1)
    whole = whole.reshape(share, count, per_block, per_block)
    return jnp.transpose(whole, (0, 2, 1, 3)).reshape(share, per_block, count * per_block)


def solution(mesh):
    placed = (P(None, None, "blk", None, "site"), P())
    return jax.shard_map(
        shards, mesh=mesh, in_specs=placed, out_specs=P("site", "blk", None), check_vma=False
    )
```

profile of v0, /device:TPU:1, one launch (start us, length us, event | category | flops | bytes accessed | tf_op | source)
XLA Modules:
  0.0 677.4 jit_solution(3509869098122849864)
XLA Ops:
  28.7 5.4 copy.142
  44.0 5.4 copy.143
  65.0 5.4 copy.144
  87.6 5.4 copy.145
  110.2 5.4 copy.146
  132.7 5.4 copy.147
  155.1 5.4 copy.148
  163.5 5.4 collective-permute-done.6
  174.2 18.7 %broadcast_multiply_fusion = (f32[1,1,16,4,4,16,4,2]{3,2,7,6,5,4,1,0:T(8,128)}, f32[1,1,16,4,4,16,4,2]{3,2,7,6,5,4,1,0:T(8,128)}, f32[1,1,16,4,4,16,4,2]{3,2,7,6...) fusion(f32[1,1,16,4,4,16,4,2]{3,2,7,6,5,4,1,0:T(8,128)} %sub.17, ...), kind=kLoop, calls=%fused_computation.1 | loop fusion | flops 229376 | bytes 1835520 | tf_op jit(solution)/shard_map/mul | solution.py:68
  192.8 5.4 copy.158
  198.2 6.1 copy.153
  204.3 6.1 copy.154
  210.5 6.1 copy.155
  216.6 6.1 copy.156
  222.7 6.1 copy.157
  228.8 6.3 copy.152
  238.8 6.1 copy.149
  252.9 6.2 reshape.787
  272.6 5.4 copy.150
  279.1 9.6 %copy.151 = f32[1,4,4,4,2,9,16,16]{7,6,4,3,2,1,5,0:T(8,128)} copy(f32[1,4,4,4,2,9,16,16]{6,7,4,2,1,3,0,5:T(8,128)} %bitcast.192) | data formatting | bytes 2359296 | tf_op jit(solution)/shard_map/transpose | solution.py:106
  288.6 7.8 %reshape.786 = f32[128,9,256]{2,0,1:T(8,128)} reshape(f32[1,4,4,4,2,9,16,16]{7,6,4,3,2,1,5,0:T(8,128)} %copy.151) | data formatting | bytes 2359296 | tf_op jit(solution)/shard_map/reshape | solution.py:106
  298.4 306.1 %all-reduce.5.cloned.1.call-done = (f32[128,9,256]{2,0,1:T(8,128)}, f32[128,7,256]{2,0,1:T(8,128)}) async-done(((f32[128,9,256]{2,0,1:T(8,128)}, f32[128,7,256]{2,0,1:T(8,128)}), (f32[128,9,256]{2,0,1:T(8,128)}, f32[128,7,256]{2,0,1:T(8,128)})) %all-reduce.5.cloned.1.call-update) | async-done | bytes 2097168
  605.3 26.1 %collective-permute-start.14 = (f32[4,256]{1,0:T(4,128)S(1)}, f32[4,256]{1,0:T(4,128)S(1)}, u32[]{:S(2)}, u32[]{:S(2)}) collective-permute-start(f32[4,256]{1,0:T(4,128)S(1)} %get-tuple-element.11), channel_id=1, source_target_pairs={{0,288},{32,320},{64,352},{96,384},{128,416},{160,448},{192,480},{... | collective-permute-start | bytes 12296 | tf_op jit(solution)/shard_map/ppermute | solution.py:16
  638.7 5.7 collective-permute-start.8
  (192 shorter events, 184.9 us)
Async XLA Ops:
  6.5 597.9 %all-reduce.5.cloned.1.call-start = ((), (), s32[]{:S(2)}) async-start(), calls=%async_computation | async-start | bytes 4194304
  7.5 27.8 %collective-permute-start = (bf16[2,1,16,4,3,128]{5,4,0,3,2,1:T(4,128)(2,1)S(1)}, bf16[2,1,16,4,3,128]{5,4,0,3,2,1:T(4,128)(2,1)S(1)}, u32[]{:S(2)}, u32[]{:S(2)}) collective-permute-start(bf16[2,1,16,4,3,128]{5,4,0,3,2,1:T(4,128)(2,1)S(1)} %copy.190), channel_id=1, source_target_pairs={{0,32},{32,64},{64,96},{96,128},{128,160},{160,192},{192,224},{224... | collective-permute-start | bytes 294920 | tf_op jit(solution)/shard_map/ppermute | solution.py:16
  49.4 6.9 %collective-permute-start.1 = (bf16[2,1,16,4,3,128]{5,4,0,3,2,1:T(4,128)(2,1)S(1)}, bf16[2,1,16,4,3,128]{5,4,0,3,2,1:T(4,128)(2,1)S(1)}, u32[]{:S(2)}, u32[]{:S(2)}) collective-permute-start(bf16[2,1,16,4,3,128]{5,4,0,3,2,1:T(4,128)(2,1)S(1)} %collective-permute-done), channel_id=1, source_target_pairs={{0,32},{32,64},{64,96},{96,128},{128,160},{160,192},{192,224},{224... | collective-permute-start | bytes 294920 | tf_op jit(solution)/shard_map/ppermute | solution.py:16
  70.5 8.4 %collective-permute-start.2 = (bf16[2,1,16,4,3,128]{5,4,0,3,2,1:T(4,128)(2,1)S(1)}, bf16[2,1,16,4,3,128]{5,4,0,3,2,1:T(4,128)(2,1)S(1)}, u32[]{:S(2)}, u32[]{:S(2)}) collective-permute-start(bf16[2,1,16,4,3,128]{5,4,0,3,2,1:T(4,128)(2,1)S(1)} %collective-permute-done.1), channel_id=1, source_target_pairs={{0,32},{32,64},{64,96},{96,128},{128,160},{160,192},{192,224},{224... | collective-permute-start | bytes 294920 | tf_op jit(solution)/shard_map/ppermute | solution.py:16
  93.0 8.4 %collective-permute-start.3 = (bf16[2,1,16,4,3,128]{5,4,0,3,2,1:T(4,128)(2,1)S(1)}, bf16[2,1,16,4,3,128]{5,4,0,3,2,1:T(4,128)(2,1)S(1)}, u32[]{:S(2)}, u32[]{:S(2)}) collective-permute-start(bf16[2,1,16,4,3,128]{5,4,0,3,2,1:T(4,128)(2,1)S(1)} %collective-permute-done.2), channel_id=1, source_target_pairs={{0,32},{32,64},{64,96},{96,128},{128,160},{160,192},{192,224},{224... | collective-permute-start | bytes 294920 | tf_op jit(solution)/shard_map/ppermute | solution.py:16
  115.6 8.4 %collective-permute-start.4 = (bf16[2,1,16,4,3,128]{5,4,0,3,2,1:T(4,128)(2,1)S(1)}, bf16[2,1,16,4,3,128]{5,4,0,3,2,1:T(4,128)(2,1)S(1)}, u32[]{:S(2)}, u32[]{:S(2)}) collective-permute-start(bf16[2,1,16,4,3,128]{5,4,0,3,2,1:T(4,128)(2,1)S(1)} %collective-permute-done.3), channel_id=1, source_target_pairs={{0,32},{32,64},{64,96},{96,128},{128,160},{160,192},{192,224},{224... | collective-permute-start | bytes 294920 | tf_op jit(solution)/shard_map/ppermute | solution.py:16
  138.1 8.4 %collective-permute-start.5 = (bf16[2,1,16,4,3,128]{5,4,0,3,2,1:T(4,128)(2,1)S(1)}, bf16[2,1,16,4,3,128]{5,4,0,3,2,1:T(4,128)(2,1)S(1)}, u32[]{:S(2)}, u32[]{:S(2)}) collective-permute-start(bf16[2,1,16,4,3,128]{5,4,0,3,2,1:T(4,128)(2,1)S(1)} %collective-permute-done.4), channel_id=1, source_target_pairs={{0,32},{32,64},{64,96},{96,128},{128,160},{160,192},{192,224},{224... | collective-permute-start | bytes 294920 | tf_op jit(solution)/shard_map/ppermute | solution.py:16
  160.5 8.4 %collective-permute-start.6 = (bf16[2,1,16,4,3,128]{5,4,0,3,2,1:T(4,128)(2,1)S(1)}, bf16[2,1,16,4,3,128]{5,4,0,3,2,1:T(4,128)(2,1)S(1)}, u32[]{:S(2)}, u32[]{:S(2)}) collective-permute-start(bf16[2,1,16,4,3,128]{5,4,0,3,2,1:T(4,128)(2,1)S(1)} %collective-permute-done.5), channel_id=1, source_target_pairs={{0,32},{32,64},{64,96},{96,128},{128,160},{160,192},{192,224},{224... | collective-permute-start | bytes 294920 | tf_op jit(solution)/shard_map/ppermute | solution.py:16
  244.9 2.9 copy-start.4
  244.9 3.0 copy-start.3
  244.9 3.1 copy-start.2
  246.4 1.7 copy-start.1
  252.9 8.1 %copy-start = (f32[1,1,16,4,4,16,4,2]{5,2,7,6,4,3,1,0:T(8,128)S(1)}, f32[1,1,16,4,4,16,4,2]{5,2,7,6,4,3,1,0:T(8,128)}, u32[]{:S(2)}) copy-start(f32[1,1,16,4,4,16,4,2]{5,2,7,6,4,3,1,0:T(8,128)} %copy.149) | copy-start | bytes 393220
  259.1 8.4 %collective-permute-start.7 = (bf16[2,1,16,4,3,128]{5,4,0,3,2,1:T(4,128)(2,1)S(1)}, bf16[2,1,16,4,3,128]{5,4,0,3,2,1:T(4,128)(2,1)S(1)}, u32[]{:S(2)}, u32[]{:S(2)}) collective-permute-start(bf16[2,1,16,4,3,128]{5,4,0,3,2,1:T(4,128)(2,1)S(1)} %collective-permute-done.6), channel_id=1, source_target_pairs={{0,32},{32,64},{64,96},{96,128},{128,160},{160,192},{192,224},{224... | collective-permute-start | bytes 294920 | tf_op jit(solution)/shard_map/ppermute | solution.py:16
  605.3 51.5 %collective-permute-start.14 = (f32[4,256]{1,0:T(4,128)S(1)}, f32[4,256]{1,0:T(4,128)S(1)}, u32[]{:S(2)}, u32[]{:S(2)}) collective-permute-start(f32[4,256]{1,0:T(4,128)S(1)} %get-tuple-element.11), channel_id=1, source_target_pairs={{0,288},{32,320},{64,352},{96,384},{128,416},{160,448},{192,480},{... | collective-permute-start | bytes 12296 | tf_op jit(solution)/shard_map/ppermute | solution.py:16
  631.3 25.4 %collective-permute-start.13 = (f32[4,256]{1,0:T(4,128)S(1)}, f32[4,256]{1,0:T(4,128)S(1)}, u32[]{:S(2)}, u32[]{:S(2)}) collective-permute-start(f32[4,256]{1,0:T(4,128)S(1)} %get-tuple-element.12), channel_id=1, source_target_pairs={{0,320},{32,352},{64,384},{96,416},{128,448},{160,480},{192,0},{22... | collective-permute-start | bytes 12296 | tf_op jit(solution)/shard_map/ppermute | solution.py:16
  634.1 22.6 %collective-permute-start.12 = (f32[4,256]{1,0:T(4,128)S(1)}, f32[4,256]{1,0:T(4,128)S(1)}, u32[]{:S(2)}, u32[]{:S(2)}) collective-permute-start(f32[4,256]{1,0:T(4,128)S(1)} %get-tuple-element.13), channel_id=1, source_target_pairs={{0,352},{32,384},{64,416},{96,448},{128,480},{160,0},{192,32},{224... | collective-permute-start | bytes 12296 | tf_op jit(solution)/shard_map/ppermute | solution.py:16
  636.0 20.7 %collective-permute-start.11 = (f32[4,256]{1,0:T(4,128)S(1)}, f32[4,256]{1,0:T(4,128)S(1)}, u32[]{:S(2)}, u32[]{:S(2)}) collective-permute-start(f32[4,256]{1,0:T(4,128)S(1)} %get-tuple-element.14), channel_id=1, source_target_pairs={{0,384},{32,416},{64,448},{96,480},{128,0},{160,32},{192,64},{224,... | collective-permute-start | bytes 12296 | tf_op jit(solution)/shard_map/ppermute | solution.py:16
  638.7 7.1 %collective-permute-start.8 = (f32[4,256]{1,0:T(4,128)S(1)}, f32[4,256]{1,0:T(4,128)S(1)}, u32[]{:S(2)}, u32[]{:S(2)}) collective-permute-start(f32[4,256]{1,0:T(4,128)S(1)} %get-tuple-element.17), channel_id=1, source_target_pairs={{0,480},{32,0},{64,32},{96,64},{128,96},{160,128},{192,160},{224,1... | collective-permute-start | bytes 12296 | tf_op jit(solution)/shard_map/ppermute | solution.py:16
  645.8 6.0 collective-permute-start.9
  651.8 4.9 collective-permute-start.10
Sparse Core Ops, SparseCore 0:
  296.6 307.8 all-reduce.4
where the time goes:
time: 688 us; the launch traced here: 677 us
  waiting for transfers between devices  344 us (50%)
  local copies, waits for them, and re-layouts  221 us (32%)
  starting transfers between devices  66.5 us (10%)
  other arithmetic  24.8 us (4%)
  between operations  15.3 us (2%)
    unnamed x2, waiting for transfers between devices  306 us
    add x18, local copies, waits for them, and re-layouts, split_terms(): return (cosine_term + sine_term, (cosine_term - sine_term) * signs)  82 us
    ppermute x15, starting transfers between devices, from_behind(): lax.ppermute(shard, axis, [(i, (i + by) % devices) for i in range(devices)])  66.5 us
    mul x7, local copies, waits for them, and re-layouts, split_terms(): return (cosine_term + sine_term, (cosine_term - sine_term) * signs)  42.3 us
    ppermute x15, waiting for transfers between devices, from_behind(): lax.ppermute(shard, axis, [(i, (i + by) % devices) for i in range(devices)])  38.3 us
    unnamed x75, local copies, waits for them, and re-layouts  28.6 us
    sub x7, local copies, waits for them, and re-layouts, split_terms(): return (cosine_term + sine_term, (cosine_term - sine_term) * signs)  25.7 us
    mul x1, other arithmetic, split_terms(): return (cosine_term + sine_term, (cosine_term - sine_term) * signs)  18.7 us
  transfers between devices with their start and end apart: 16, of which 11 were waited for; matrix products, arithmetic and copies ran while one was open for 5% of the time, Pallas kernels for 0%

commit v1 on v0

v1 whole, which is shorter than its diff:
```python
import math

import jax
import jax.numpy as jnp
from jax import lax
from jax.experimental import pallas as pl
from jax.experimental.pallas import tpu as pltpu
from jax.sharding import PartitionSpec as P

LEXT = 48
TWO_PI = 2.0 * math.pi
MESH = pl.DeviceIdType.MESH
F32 = jnp.float32
BF16 = jnp.bfloat16
ZTYPE = jnp.bfloat16

NX, NY, NZ, NH = 4, 8, 8, 4
KEY = 768


def device(x, y, z, core):
    blk = x * 4 + lax.rem(y, 2) * 2 + core
    site = z * 4 + lax.div(y, 2)
    return (blk, site)


def remote(src, dst, send_sem, recv_sem, target):
    return pltpu.make_async_remote_copy(
        src_ref=src, dst_ref=dst, send_sem=send_sem, recv_sem=recv_sem,
        device_id=target, device_id_type=MESH,
    )


def kernel(
    modes_ref, mom_ref, out_ref,
    rows, cols, right_hi, right_lo, acc, tmp, zsend, zrecv, red, frecv,
    ring_s, ring_r, sib_s, sib_r, x_s, x_r, z_s, z_r, f_s, f_r,
):
    blk = lax.axis_index("blk")
    site = lax.axis_index("site")
    x = lax.div(blk, 4)
    yl = lax.rem(lax.div(blk, 2), 2)
    core = lax.rem(blk, 2)
    z = lax.div(site, 4)
    rho = lax.rem(site, 4)
    y = rho * 2 + yl
    other = 1 - core

    barrier = pltpu.get_barrier_semaphore()
    count = 0
    partners = []
    for dy in range(NY):
        for dc in range(2):
            if dy or dc:
                partners.append(device(x, lax.rem(y + dy, NY), z, lax.rem(core + dc, 2)))
    for dx in range(1, NX):
        partners.append(device(lax.rem(x + dx, NX), y, z, core))
    for dz in range(1, NZ):
        partners.append(device(x, y, lax.rem(z + dz, NZ), core))
    for target in partners:
        pl.semaphore_signal(barrier, inc=1, device_id=target, device_id_type=MESH)

    for c in range(2):
        for i in range(16):
            tmp[c, pl.ds(16 * i, 12), :] = modes_ref[c, 0, i].astype(F32)
    for c in range(2):
        for s in range(4):
            for a in range(3):
                piece = tmp[c, pl.ds(3 * s + a, 16, stride=16), :]
                lane = (c * 3 + a) * 128
                rows[y, core, pl.ds(16 * s, 16), pl.ds(lane, 128)] = piece.astype(BF16)

    row = lax.broadcasted_iota(jnp.int32, (8, 128), 0)
    lane = lax.broadcasted_iota(jnp.int32, (8, 128), 1)
    flat = ((z * 4 + (row & 3)) * 128 + lane).astype(F32)
    plane = jnp.floor((flat + 0.5) * (1.0 / (LEXT * LEXT)))
    line = jnp.floor((flat + 0.5) * (1.0 / LEXT))
    coords = (flat - LEXT * line, line - LEXT * plane, plane)
    phases = []
    for k in range(4):
        turns = sum(mom_ref[k, d].astype(F32) * coords[d] for d in range(3))
        turns = turns - LEXT * jnp.floor((turns + 0.5) * (1.0 / LEXT))
        angle = turns * (TWO_PI / LEXT)
        phases.append((jnp.cos(angle), jnp.sin(angle)))
    for k in range(4):
        tmp[0, pl.ds(8 * k, 8), :] = phases[k][0]
        tmp[1, pl.ds(8 * k, 8), :] = phases[k][1]

    pl.semaphore_wait(barrier, len(partners))

    sign = (1, NY - 1)

    def ring(d, t, h):
        src = rows.at[lax.rem(y + (NY - sign[d]) * (t - 1), NY), core, pl.ds(32 * h, 32), :]
        target = device(x, lax.rem(y + sign[d], NY), z, core)
        return remote(src, src, ring_s.at[d, t - 1, h], ring_r.at[d, t - 1, h], target)

    def ring_in(d, t, h):
        dst = rows.at[lax.rem(y + (NY - sign[d]) * t, NY), core, pl.ds(32 * h, 32), :]
        target = device(x, lax.rem(y + sign[d], NY), z, core)
        return remote(dst, dst, ring_s.at[d, t - 1, h], ring_r.at[d, t - 1, h], target)

    def place(d, t):
        return 0 if t == 0 else 1 + d * 4 + t - 1

    def sib(d, t, h):
        src = rows.at[lax.rem(y + (NY - sign[d]) * t, NY), core, pl.ds(32 * h, 32), :]
        at = place(d, t)
        return remote(src, src, sib_s.at[at, h], sib_r.at[at, h], device(x, y, z, other))

    def sib_in(d, t, h):
        dst = rows.at[lax.rem(y + (NY - sign[d]) * t, NY), other, pl.ds(32 * h, 32), :]
        at = place(d, t)
        return remote(dst, dst, sib_s.at[at, h], sib_r.at[at, h], device(x, y, z, other))

    def x_out(dx, e):
        hi = lax.rem(rho + e, NH)
        src = rows.at[hi * 2 + yl, core, pl.ds(pl.multiple_of(rho * 16, 16), 16), :]
        target = device(lax.rem(x + dx, NX), y, z, core)
        return remote(src, cols.at[x, hi], x_s.at[dx - 1, e], x_r.at[dx - 1, e], target)

    def x_in(dx, e):
        hi = lax.rem(rho + e, NH)
        dst = cols.at[lax.rem(x + NX - dx, NX), hi]
        target = device(lax.rem(x + dx, NX), y, z, core)
        return remote(dst, dst, x_s.at[dx - 1, e], x_r.at[dx - 1, e], target)

    def x_start(e):
        for dx in (2, 1, 3):
            x_out(dx, e).start()
        hi = lax.rem(rho + e, NH)
        cols[x, hi] = rows[hi * 2 + yl, core, pl.ds(pl.multiple_of(rho * 16, 16), 16), :]

    def multiply(e):
        hi = lax.rem(rho + e, NH)
        for dx in range(1, NX):
            x_in(dx, e).wait_recv()
        for k in range(4):
            cos = tmp[0, pl.ds(8 * k + hi, 1), :]
            sin = tmp[1, pl.ds(8 * k + hi, 1), :]
            for xs in range(NX):
                for a in range(3):
                    ur = cols[xs, hi, :, pl.ds(a * 128, 128)].astype(F32)
                    ui = cols[xs, hi, :, pl.ds((3 + a) * 128, 128)].astype(F32)
                    qr = ur * cos + ui * sin
                    qi = ui * cos - ur * sin
                    hr, hm = qr.astype(BF16), qi.astype(BF16)
                    lr = (qr - hr.astype(F32)).astype(BF16)
                    lm = (qi - hm.astype(F32)).astype(BF16)
                    at = k * 128 + (xs % 2) * 64 + (xs // 2) * 16
                    for buffer, re, im in ((right_hi, hr, hm), (right_lo, lr, lm)):
                        buffer[pl.ds(at, 16), pl.ds(a * 128, 128)] = re
                        buffer[pl.ds(at, 16), pl.ds((3 + a) * 128, 128)] = im
                        buffer[pl.ds(at + 32, 16), pl.ds(a * 128, 128)] = im
                        buffer[pl.ds(at + 32, 16), pl.ds((3 + a) * 128, 128)] = -re
        dims = (((1,), (1,)), ((), ()))
        left = rows[pl.ds(hi * 2, 2)].reshape(256, KEY)
        for k in range(4):
            part = lax.dot_general(left, right_hi[pl.ds(128 * k, 128), :], dims, preferred_element_type=F32)
            part += lax.dot_general(left, right_lo[pl.ds(128 * k, 128), :], dims, preferred_element_type=F32)
            if e == 0:
                acc[k] = part
            else:
                acc[k] += part

    started = []
    for h in range(2):
        for d in range(2):
            ring(d, 1, h).start()
    for h in range(2):
        sib(0, 0, h).start()
    x_start(0)
    for h in range(2):
        for d in range(2):
            ring_in(d, 1, h).wait_recv()
            ring(d, 2, h).start()
            sib(d, 1, h).start()
    for h in range(2):
        for d in range(2):
            ring_in(d, 2, h).wait_recv()
            ring(d, 3, h).start()
            sib(d, 2, h).start()
    x_start(1)
    x_start(3)
    for h in range(2):
        sib_in(0, 0, h).wait_recv()
        for d in range(2):
            sib_in(d, 1, h).wait_recv()
    multiply(0)
    for h in range(2):
        for d in range(2):
            ring_in(d, 3, h).wait_recv()
            if h == d:
                ring(d, 4, h).start()
            sib(d, 3, h).start()
    for h in range(2):
        for d in range(2):
            sib_in(d, 2, h).wait_recv()
            sib_in(d, 3, h).wait_recv()
    multiply(1)
    for d in range(2):
        ring_in(d, 4, d).wait_recv()
        sib(d, 4, d).start()
    x_start(2)
    multiply(3)
    for d in range(2):
        sib_in(d, 4, d).wait_recv()
    multiply(2)

    for zz in range(NZ):
        for q in range(4):
            zsend[zz, pl.ds(32 * q, 32), :] = acc[zz // 2, pl.ds(64 * q + 32 * (zz % 2), 32), :].astype(ZTYPE)

    def z_out(dz):
        to = lax.rem(z + dz, NZ)
        return remote(zsend.at[to], zrecv.at[dz - 1], z_s.at[dz - 1], z_r.at[dz - 1], device(x, y, to, core))

    for dz in (4, 3, 5, 2, 6, 1, 7):
        z_out(dz).start()
    half = pl.multiple_of(lax.rem(z, 2) * 32, 32)
    for q in range(4):
        red[pl.ds(32 * q, 32), :] = acc[lax.div(z, 2), pl.ds(64 * q + half, 32), :]
    for dz in (1, 7, 2, 6, 3, 5, 4):
        z_out(dz).wait_recv()
        red[...] += zrecv[dz - 1].astype(F32)

    mine = lax.rem(rho, 2) * 4 + yl * 2 + core

    def f_out(q, sp):
        to = device(x, (sp * 2 + lax.div(rho, 2)) * 2 + q // 2, z, q % 2)
        src = red.at[pl.ds(32 * q + 16 * sp, 16), :]
        return remote(src, frecv.at[mine], f_s.at[q * 2 + sp], f_r.at[mine], to)

    def f_self(q, sp):
        return (sp * 2 + lax.div(rho, 2) == rho) & (yl == q // 2) & (core == q % 2)

    def f_in(b, q):
        dst = frecv.at[b * 4 + q]
        source = device(x, (lax.rem(rho, 2) * 2 + b) * 2 + q // 2, z, q % 2)
        return remote(dst, dst, f_s.at[b * 4 + q], f_r.at[b * 4 + q], source)

    def f_self_in(b, q):
        return (lax.rem(rho, 2) * 2 + b == rho) & (yl == q // 2) & (core == q % 2)

    for sp in range(2):
        for q in range(4):
            here = f_self(q, sp)

            @pl.when(jnp.logical_not(here))
            def _():
                f_out(q, sp).start()

            @pl.when(here)
            def _():
                frecv[mine] = red[pl.ds(32 * q + 16 * sp, 16), :]

    for b in range(2):
        for q in range(4):

            @pl.when(jnp.logical_not(f_self_in(b, q)))
            def _():
                f_in(b, q).wait_recv()

    group = lax.div(lax.rem(lax.broadcasted_iota(jnp.int32, (16, 128), 1), 64), 16)
    for b in range(2):
        pieces = [frecv[b * 4 + q] for q in range(4)]
        for c in range(2):
            for v in range(2):
                m = c * 2 + v
                total = pieces[m]
                for q in range(4):
                    if q != m:
                        moved = pltpu.roll(pieces[q], ((q - m) * 16) % 128, 1)
                        total = jnp.where(group == q, moved, total)
                out_ref[b * 2 + c, :, pl.ds(128 * v, 128)] = total

    for h in range(2):
        sib(0, 0, h).wait_send()
        for d in range(2):
            for t in (1, 2, 3):
                ring(d, t, h).wait_send()
                sib(d, t, h).wait_send()
    for d in range(2):
        ring(d, 4, d).wait_send()
        sib(d, 4, d).wait_send()
    for e in range(4):
        for dx in range(1, NX):
            x_out(dx, e).wait_send()
    for dz in range(1, NZ):
        z_out(dz).wait_send()
    for sp in range(2):
        for q in range(4):

            @pl.when(jnp.logical_not(f_self(q, sp)))
            def _():
                f_out(q, sp).wait_send()


def shards(modes, momenta):
    dma = pltpu.SemaphoreType.DMA
    return pl.pallas_call(
        kernel,
        out_shape=jax.ShapeDtypeStruct((4, 16, 256), F32),
        in_specs=[
            pl.BlockSpec(memory_space=pltpu.VMEM),
            pl.BlockSpec(memory_space=pltpu.SMEM),
        ],
        out_specs=pl.BlockSpec(memory_space=pltpu.VMEM),
        scratch_shapes=[
            pltpu.VMEM((NY, 2, 64, KEY), BF16),
            pltpu.VMEM((NX, NH, 16, KEY), BF16),
            pltpu.VMEM((512, KEY), BF16),
            pltpu.VMEM((512, KEY), BF16),
            pltpu.VMEM((4, 256, 128), F32),
            pltpu.VMEM((2, 256, 128), F32),
            pltpu.VMEM((NZ, 128, 128), ZTYPE),
            pltpu.VMEM((NZ - 1, 128, 128), ZTYPE),
            pltpu.VMEM((128, 128), F32),
            pltpu.VMEM((8, 16, 128), F32),
            dma((2, 4, 2)), dma((2, 4, 2)),
            dma((9, 2)), dma((9, 2)),
            dma((NX - 1, NH)), dma((NX - 1, NH)),
            dma((NZ - 1,)), dma((NZ - 1,)),
            dma((8,)), dma((8,)),
        ],
        compiler_params=pltpu.CompilerParams(
            collective_id=0, has_side_effects=True, vmem_limit_bytes=32 * 1024 * 1024
        ),
    )(modes, momenta)


def solution(mesh):
    placed = (P(None, None, "blk", None, "site"), P())
    return jax.shard_map(
        shards, mesh=mesh, in_specs=placed, out_specs=P("site", "blk", None), check_vma=False
    )
```

time: 688 us -> 49 us (0.07); the launches traced: 677 us -> 48.9 us
  waiting for transfers between devices: 344 us -> 0 us
  local copies, waits for them, and re-layouts: 221 us -> 1.57 us
  starting transfers between devices: 66.5 us -> 0 us
  Pallas kernels: 0 us -> 47.3 us
  other arithmetic: 24.8 us -> 0 us
  between operations: 15.3 us -> 0.02 us
    unnamed x2 -> x0, waiting for transfers between devices: 306 us -> none
    add x18 -> x0, local copies, waits for them, and re-layouts: 82 us -> none  [split_terms(): return (cosine_term + sine_term, (cosine_term - sine_term) * signs)]
    ppermute x15 -> x0, starting transfers between devices: 66.5 us -> none  [from_behind(): lax.ppermute(shard, axis, [(i, (i + by) % devices) for i in range(devices)])]
    pallas_call x0 -> x1, Pallas kernels: none -> 47.3 us  [shards(): pl.pallas_call(kernel, out_shape=jax.ShapeDtypeStruct((4, 16, 256), F32),...]
    mul x7 -> x0, local copies, waits for them, and re-layouts: 42.3 us -> none  [split_terms(): return (cosine_term + sine_term, (cosine_term - sine_term) * signs)]
    ppermute x15 -> x0, waiting for transfers between devices: 38.3 us -> none  [from_behind(): lax.ppermute(shard, axis, [(i, (i + by) % devices) for i in range(devices)])]
    unnamed x75 -> x4, local copies, waits for them, and re-layouts: 28.6 us -> 1.57 us
    sub x7 -> x0, local copies, waits for them, and re-layouts: 25.7 us -> none  [split_terms(): return (cosine_term + sine_term, (cosine_term - sine_term) * signs)]
  transfers between devices with their start and end apart: 16 -> 0, of which waited for: 11 -> 0; matrix products, arithmetic and copies ran while one was open for 5% -> 0% of each run, Pallas kernels for 0% -> 0%
where the time goes in v1:
time: 49 us; the launch traced here: 48.9 us
  Pallas kernels  47.3 us (97%)
  local copies, waits for them, and re-layouts  1.57 us (3%)
    pallas_call x1, Pallas kernels, shards(): pl.pallas_call(kernel, out_shape=jax.ShapeDtypeStruct((4, 16, 256), F32),...  47.3 us
    unnamed x4, local copies, waits for them, and re-layouts  1.57 us

profile of v1, /device:TPU:1, one launch (start us, length us, event | category | flops | bytes accessed | tf_op | source)
XLA Modules:
  0.0 48.9 jit_solution(4985439308172413163)
XLA Ops:
  0.0 0.0 copy-start
  0.0 0.9 %copy.3.modes_ref = bf16[2,1,16,12,128]{4,3,2,1,0:T(8,128)(2,1)S(1)} copy(bf16[2,1,16,12,128]{4,2,3,1,0:T(8,128)(2,1)} %param.2) | data formatting | bytes 196608 | tf_op args[0]
  0.9 0.0 copy-done
  1.0 47.3 %shard_map.28 = f32[4,16,256]{2,1,0:T(8,128)S(1)} custom-call(bf16[2,1,16,12,128]{4,3,2,1,0:T(8,128)(2,1)S(1)} %copy.3.modes_ref, s32[4,3]{1,0:T(4,128)S(1)} %copy-done), custom_call_target="tpu_custom_call" | custom-call | tf_op jit(solution)/shard_map/pallas_call | solution.py:301
  48.2 0.6 %copy.5 = f32[4,16,256]{2,1,0:T(8,128)} copy(f32[4,16,256]{2,1,0:T(8,128)S(1)} %shard_map.28) | data formatting | bytes 131072
Async XLA Ops:
  0.0 0.9 %copy-start = (s32[4,3]{1,0:T(4,128)S(1)}, s32[4,3]{1,0:T(4,128)}, u32[]{:S(2)}) copy-start(s32[4,3]{1,0:T(4,128)} %mom_ref.1) | copy-start | bytes 148

commit v2 on v0

v2 whole, which is shorter than its diff:
```python
import math

import jax
import jax.numpy as jnp
from jax import lax
from jax.experimental import pallas as pl
from jax.experimental.pallas import tpu as pltpu
from jax.sharding import PartitionSpec as P

LEXT = 48
TWO_PI = 2.0 * math.pi
MESH = pl.DeviceIdType.MESH
F32 = jnp.float32
BF16 = jnp.bfloat16

NX, NZ, NH = 4, 8, 4
KEY = 768
ROWS = (((1,), (1,)), ((), ()))


def remote(src, dst, send_sem, recv_sem, target):
    return pltpu.make_async_remote_copy(
        src_ref=src, dst_ref=dst, send_sem=send_sem, recv_sem=recv_sem,
        device_id=target, device_id_type=MESH,
    )


def spin_of(hi):
    return (1 - lax.rem(hi, 2)) * 2 + lax.div(hi, 2)


def spin_rows(spin):
    return pl.ds(pl.multiple_of(spin * 16, 16), 16)


def kernel(
    modes_ref, mom_ref, out_ref,
    stage, mom, rows, cols, left_hi, left_lo, acc, wave, zsend, zrecv, red,
    in_s, y_s, y_r, o_s, o_r, x_s, x_r, s_s, s_r, z_s, z_r, f_s, f_r,
):
    blk = lax.axis_index("blk")
    site = lax.axis_index("site")
    x = lax.div(blk, 4)
    yl = lax.rem(lax.div(blk, 2), 2)
    core = lax.rem(blk, 2)
    z = lax.div(site, 4)
    rho = lax.rem(site, 4)
    spin = spin_of(rho)

    def device(x, yl, core, z, hi):
        return (x * 4 + yl * 2 + core, z * 4 + hi)

    def block(x, yl, core):
        return x * 4 + yl * 2 + core

    def lane_of(o):
        return yl if o == 0 else 1 - yl

    def up(hi, e):
        return lax.rem(hi + e, NH)

    barrier = pltpu.get_barrier_semaphore()
    partners = [device(x, lane_of(o), core, z, up(rho, e)) for e in range(NH) for o in range(2) if e or o]
    partners += [device(lax.rem(x + dx, NX), yl, core, z, rho) for dx in range(1, NX)]
    partners += [device(x, yl, core, lax.rem(z + dz, NZ), rho) for dz in range(1, NZ)]
    partners += [device(x, yl, 1 - core, z, rho)]
    for target in partners:
        pl.semaphore_signal(barrier, inc=1, device_id=target, device_id_type=MESH)
    get_modes = pltpu.make_async_copy(modes_ref, stage, in_s.at[0])
    get_modes.start()
    get_mom = pltpu.make_async_copy(mom_ref, mom, in_s.at[1])
    get_mom.start()

    get_modes.wait()
    for c in range(2):
        for s in range(4):
            for a in range(3):
                rows[rho, pl.ds(16 * s, 16), pl.ds((c * 3 + a) * 128, 128)] = stage[c, 0, 3 * s + a]
    cols[rho, blk] = rows[rho, spin_rows(spin), :]

    def y_out(e, j):
        to = up(rho, e)
        piece = rows.at[rho, spin_rows(lax.rem(spin_of(to) + j, 4)), :]
        return remote(piece, piece, y_s.at[e - 1, j], y_r.at[e - 1, j], device(x, yl, core, z, to))

    def y_in(e, j):
        piece = rows.at[up(rho, NH - e), spin_rows(lax.rem(spin + j, 4)), :]
        return remote(piece, piece, y_s.at[e - 1, j], y_r.at[e - 1, j], device(x, yl, core, z, up(rho, NH - e)))

    def o_out(e):
        to = up(rho, e)
        piece = rows.at[rho, spin_rows(spin_of(to)), :]
        return remote(piece, cols.at[rho, blk], o_s.at[e], o_r.at[e], device(x, 1 - yl, core, z, to))

    def o_in(e):
        hi = up(rho, NH - e)
        piece = cols.at[hi, block(x, 1 - yl, core)]
        return remote(piece, piece, o_s.at[e], o_r.at[e], device(x, 1 - yl, core, z, hi))

    def x_out(dx, e, o):
        piece = cols.at[up(rho, NH - e), block(x, lane_of(o), core)]
        to = device(lax.rem(x + dx, NX), yl, core, z, rho)
        return remote(piece, piece, x_s.at[dx - 1, e, o], x_r.at[dx - 1, e, o], to)

    def x_in(dx, e, o):
        far = lax.rem(x + NX - dx, NX)
        piece = cols.at[up(rho, NH - e), block(far, lane_of(o), core)]
        return remote(piece, piece, x_s.at[dx - 1, e, o], x_r.at[dx - 1, e, o], device(far, yl, core, z, rho))

    def s_copy(dx, e, o, side):
        far = lax.rem(x + NX - dx, NX)
        piece = cols.at[up(rho, NH - e), block(far, lane_of(o), side)]
        return remote(piece, piece, s_s.at[dx, e, o], s_r.at[dx, e, o], device(x, yl, 1 - core, z, rho))

    def spread(e, o):
        for dx in (2, 1, 3):
            x_out(dx, e, o).start()
        s_copy(0, e, o, core).start()

    pl.semaphore_wait(barrier, len(partners))
    y_out(2, 0).start()
    o_out(2).start()
    for e in (1, 3):
        o_out(e).start()
        y_out(e, 0).start()
    o_out(0).start()
    spread(0, 0)
    for j in range(1, 4):
        for e in (2, 1, 3):
            y_out(e, j).start()

    get_mom.wait()
    row = lax.broadcasted_iota(jnp.int32, (8, 128), 0)
    lane = lax.broadcasted_iota(jnp.int32, (8, 128), 1)
    flat = ((z * 4 + (row & 3)) * 128 + lane).astype(F32)
    plane = jnp.floor((flat + 0.5) * (1.0 / (LEXT * LEXT)))
    line = jnp.floor((flat + 0.5) * (1.0 / LEXT))
    coords = (flat - LEXT * line, line - LEXT * plane, plane)
    for k in range(4):
        turns = sum(mom[k, d].astype(F32) * coords[d] for d in range(3))
        turns = turns - LEXT * jnp.floor((turns + 0.5) * (1.0 / LEXT))
        angle = turns * (TWO_PI / LEXT)
        wave[0, pl.ds(8 * k, 8), :] = jnp.cos(angle)
        wave[1, pl.ds(8 * k, 8), :] = jnp.sin(angle)

    def prepare(e):
        hi = up(rho, NH - e)
        for k in range(4):
            cos = wave[0, pl.ds(8 * k + hi, 1), :]
            sin = wave[1, pl.ds(8 * k + hi, 1), :]
            for s in range(4):
                for a in range(3):
                    ur = rows[hi, pl.ds(16 * s, 16), pl.ds(a * 128, 128)].astype(F32)
                    ui = rows[hi, pl.ds(16 * s, 16), pl.ds((3 + a) * 128, 128)].astype(F32)
                    re = ur * cos - ui * sin
                    im = ui * cos + ur * sin
                    re_hi, im_hi = re.astype(BF16), im.astype(BF16)
                    re_lo = (re - re_hi.astype(F32)).astype(BF16)
                    im_lo = (im - im_hi.astype(F32)).astype(BF16)
                    at = k * 128 + s * 32
                    for left, first, second in ((left_hi, re_hi, im_hi), (left_lo, re_lo, im_lo)):
                        left[e, pl.ds(at, 16), pl.ds(a * 128, 128)] = first
                        left[e, pl.ds(at, 16), pl.ds((3 + a) * 128, 128)] = second
                        left[e, pl.ds(at + 16, 16), pl.ds(a * 128, 128)] = -second
                        left[e, pl.ds(at + 16, 16), pl.ds((3 + a) * 128, 128)] = first

    def multiply(e, last=False):
        right = cols[up(rho, NH - e)].reshape(256, KEY)
        for k in range(4):
            at = pl.ds(128 * k, 128)
            part = lax.dot_general(left_hi[e, at, :], right, ROWS, preferred_element_type=F32)
            part += lax.dot_general(left_lo[e, at, :], right, ROWS, preferred_element_type=F32)
            if e != 0:
                part += acc[at, :]
            acc[at, :] = part
            if last:
                zsend[2 * k] = part[:64].astype(BF16)
                zsend[2 * k + 1] = part[64:].astype(BF16)

    def relay(e, o):
        for dx in (1, 3, 2):
            x_in(dx, e, o).wait_recv()
            s_copy(dx, e, o, core).start()

    def whole(e):
        for dx in range(NX):
            for o in range(2):
                s_copy(dx, e, o, 1 - core).wait_recv()

    prepare(0)
    o_in(0).wait_recv()
    spread(0, 1)
    for e in (1, 3):
        o_in(e).wait_recv()
        spread(e, 1)
        y_in(e, 0).wait_recv()
        cols[up(rho, NH - e), blk] = rows[up(rho, NH - e), spin_rows(spin), :]
        spread(e, 0)
    o_in(2).wait_recv()
    spread(2, 1)
    y_in(2, 0).wait_recv()
    cols[up(rho, 2), blk] = rows[up(rho, 2), spin_rows(spin), :]
    spread(2, 0)
    relay(0, 0)
    relay(0, 1)
    for e in (1, 3):
        for j in range(1, 4):
            y_in(e, j).wait_recv()
        prepare(e)
        relay(e, 1)
        relay(e, 0)
    relay(2, 1)
    relay(2, 0)
    whole(0)
    multiply(0)
    for j in range(1, 4):
        y_in(2, j).wait_recv()
    prepare(2)
    for e in (1, 3):
        whole(e)
        multiply(e)
    whole(2)
    multiply(2, last=True)

    def z_out(dz):
        to = lax.rem(z + dz, NZ)
        return remote(zsend.at[to], zrecv.at[dz - 1], z_s.at[dz - 1], z_r.at[dz - 1], device(x, yl, core, to, rho))

    for dz in (4, 3, 5, 2, 6, 1, 7):
        z_out(dz).start()
    total = acc[pl.ds(pl.multiple_of(64 * z, 64), 64), :]
    for dz in (1, 7, 2, 6, 3, 5, 4):
        z_out(dz).wait_recv()
        total += zrecv[dz - 1].astype(F32)
    for sp in range(2):
        for c in range(2):
            red[sp, c] = total[32 * sp + 16 * c:32 * sp + 16 * c + 16]

    def f_out(sp):
        to = device(x, yl, core, z, sp * 2 + 1 - lax.rem(rho, 2))
        half = lax.div(rho, 2)
        return remote(red.at[sp], out_ref.at[pl.ds(half * 2, 2)], f_s.at[sp], f_r.at[half], to)

    def f_in(half):
        source = device(x, yl, core, z, half * 2 + 1 - lax.rem(rho, 2))
        piece = out_ref.at[pl.ds(half * 2, 2)]
        return remote(piece, piece, f_s.at[half], f_r.at[half], source)

    for sp in range(2):
        f_out(sp).start()

    for e in range(NH):
        o_out(e).wait_send()
        for o in range(2):
            for dx in range(1, NX):
                x_out(dx, e, o).wait_send()
            for dx in range(NX):
                s_copy(dx, e, o, core).wait_send()
        if e:
            for j in range(4):
                y_out(e, j).wait_send()
    for dz in range(1, NZ):
        z_out(dz).wait_send()
    for half in range(2):
        f_in(half).wait_recv()
    for sp in range(2):
        f_out(sp).wait_send()


def shards(modes, momenta):
    dma = pltpu.SemaphoreType.DMA
    return pl.pallas_call(
        kernel,
        out_shape=jax.ShapeDtypeStruct((4, 16, 256), F32),
        in_specs=[
            pl.BlockSpec(memory_space=pl.ANY),
            pl.BlockSpec(memory_space=pl.ANY),
        ],
        out_specs=pl.BlockSpec(memory_space=pltpu.VMEM),
        scratch_shapes=[
            pltpu.VMEM((2, 1, 12, 16, 128), BF16),
            pltpu.SMEM((4, 3), jnp.int32),
            pltpu.VMEM((NH, 64, KEY), BF16),
            pltpu.VMEM((NH, 16, 16, KEY), BF16),
            pltpu.VMEM((NH, 512, KEY), BF16),
            pltpu.VMEM((NH, 512, KEY), BF16),
            pltpu.VMEM((512, 256), F32),
            pltpu.VMEM((2, 32, 128), F32),
            pltpu.VMEM((NZ, 64, 256), BF16),
            pltpu.VMEM((NZ - 1, 64, 256), BF16),
            pltpu.VMEM((2, 2, 16, 256), F32),
            dma((2,)),
            dma((NH - 1, 4)), dma((NH - 1, 4)),
            dma((NH,)), dma((NH,)),
            dma((NX - 1, NH, 2)), dma((NX - 1, NH, 2)),
            dma((NX, NH, 2)), dma((NX, NH, 2)),
            dma((NZ - 1,)), dma((NZ - 1,)),
            dma((2,)), dma((2,)),
        ],
        compiler_params=pltpu.CompilerParams(
            collective_id=0, has_side_effects=True, vmem_limit_bytes=56 * 1024 * 1024
        ),
    )(jnp.transpose(modes, (0, 1, 3, 2, 4)), momenta)


def solution(mesh):
    placed = (P(None, None, "blk", None, "site"), P())
    return jax.shard_map(
        shards, mesh=mesh, in_specs=placed, out_specs=P("site", "blk", None), check_vma=False
    )
```

time: 688 us -> 46.9 us (0.07)
  the two profiles are of different devices: /device:TPU:1 before, /device:TPU:4 now
where the time goes in v2:
time: 46.9 us; the launch traced here: 46.7 us
  Pallas kernels  45.2 us (96%)
  local copies, waits for them, and re-layouts  1.47 us (3%)
    pallas_call x1, Pallas kernels, shards(): pl.pallas_call(kernel, out_shape=jax.ShapeDtypeStruct((4, 16, 256), F32),...  45.2 us
    unnamed x1, local copies, waits for them, and re-layouts  1.47 us

profile of v2, /device:TPU:4, one launch (start us, length us, event | category | flops | bytes accessed | tf_op | source)
XLA Modules:
  0.0 46.7 jit_solution(13717524707558199130)
XLA Ops:
  0.0 45.2 %shard_map.28 = f32[4,16,256]{2,1,0:T(8,128)} custom-call(bf16[2,1,12,16,128]{4,3,2,1,0:T(8,128)(2,1)} %bitcast.1, s32[4,3]{1,0:T(4,128)} %mom_ref.1), custom_call_target="tpu_custom_call" | custom-call | tf_op jit(solution)/shard_map/pallas_call | solution.py:272
  45.3 1.5 %copy.4 = f32[4,16,256]{2,1,0:T(8,128)} copy(f32[4,16,256]{2,1,0:T(8,128)} %shard_map.28) | data formatting | bytes 131072

commit v3 on v2

v3 whole, which is shorter than its diff:
```python
import math

import jax
import jax.numpy as jnp
from jax import lax
from jax.experimental import pallas as pl
from jax.experimental.pallas import tpu as pltpu
from jax.sharding import PartitionSpec as P

LEXT = 48
TWO_PI = 2.0 * math.pi
MESH = pl.DeviceIdType.MESH
F32 = jnp.float32
BF16 = jnp.bfloat16

NX, NZ, NH = 4, 8, 4
KEY = 768
ROWS = (((1,), (1,)), ((), ()))


def remote(src, dst, send_sem, recv_sem, target):
    return pltpu.make_async_remote_copy(
        src_ref=src, dst_ref=dst, send_sem=send_sem, recv_sem=recv_sem,
        device_id=target, device_id_type=MESH,
    )


def flip(place):
    return place + 1 - 2 * lax.rem(place, 2)


def spin_rows(spin):
    return pl.ds(pl.multiple_of(spin * 16, 16), 16)


def kernel(
    modes_ref, mom_ref, out_ref,
    stage, mom, rows, cols, left_hi, left_lo, acc, wave, zsend, zrecv,
    hand, in_s, g_s, g_r, a_s, a_r, x_s, x_r, s_s, s_r, z_s, z_r,
):
    blk = lax.axis_index("blk")
    site = lax.axis_index("site")
    x = lax.div(blk, 4)
    yl = lax.rem(lax.div(blk, 2), 2)
    core = lax.rem(blk, 2)
    z = lax.div(site, 4)
    rho = lax.rem(site, 4)

    def hi_of(e):
        return flip(rho) if e % 2 else rho

    def z_of(e):
        return flip(z) if e // 2 else z

    def spin_of(e):
        return (1 - lax.rem(hi_of(e), 2)) * 2 + lax.rem(z_of(e), 2)

    spin = spin_of(0)

    def device(x, yl, core, z, hi):
        return (x * 4 + yl * 2 + core, z * 4 + hi)

    def block(x, yl, core):
        return x * 4 + yl * 2 + core

    def lane_of(o):
        return yl if o == 0 else 1 - yl

    barrier = pltpu.get_barrier_semaphore()
    partners = [device(x, yl, 1 - core, z, rho), device(x, yl, core, z_of(3), hi_of(3))]
    partners += [device(lax.rem(x + dx, NX), yl, core, z, rho) for dx in range(1, NX)]
    partners += [device(x, 1 - yl, core, z_of(e), hi_of(e)) for e in range(NH)]
    along_z = [device(x, yl, core, lax.rem(z + dz, NZ), rho) for dz in (1, NZ - 1)]
    along_y = [device(x, yl, core, z, lax.rem(rho + dh, NH)) for dh in (1, NH - 1)]
    partners += along_z + along_y
    for target in partners:
        pl.semaphore_signal(barrier, inc=1, device_id=target, device_id_type=MESH)
    get_modes = pltpu.make_async_copy(modes_ref, stage, in_s.at[0])
    get_modes.start()
    get_mom = pltpu.make_async_copy(mom_ref, mom, in_s.at[1])
    get_mom.start()

    get_modes.wait()
    for c in range(2):
        for s in range(4):
            for a in range(3):
                rows[0, pl.ds(16 * s, 16), pl.ds((c * 3 + a) * 128, 128)] = stage[c, 0, 3 * s + a]

    def gather(e, spin_e, e_from, to, way=0):
        return remote(
            rows.at[e_from, spin_rows(spin_e), :], rows.at[e, spin_rows(spin_e), :],
            g_s.at[e - 1 + way, spin_e], g_r.at[e - 1, spin_e], to,
        )

    def y_out(j):
        return gather(1, spin_of(j), 0, device(x, yl, core, z, flip(rho)))

    def z_out(j):
        return gather(2, spin_of(j), 0, device(x, yl, core, flip(z), rho))

    def d_out():
        return gather(3, spin_of(3), 0, device(x, yl, core, z_of(3), hi_of(3)), 1)

    def f_out(j):
        return gather(3, spin_of(j), 1, device(x, yl, core, flip(z), rho))

    def g_in(e, j):
        to = device(x, yl, core, flip(z), rho) if e > 1 else device(x, yl, core, z, flip(rho))
        return gather(e, spin_of(j), e, to)

    def a_out(e):
        to = device(x, 1 - yl, core, z_of(e), hi_of(e))
        return remote(rows.at[0, spin_rows(spin_of(e)), :], cols.at[e, blk], a_s.at[e], a_r.at[e], to)

    def a_in(e):
        piece = cols.at[e, block(x, 1 - yl, core)]
        return remote(piece, piece, a_s.at[e], a_r.at[e], device(x, 1 - yl, core, z_of(e), hi_of(e)))

    def x_out(dx, e, o):
        piece = cols.at[e, block(x, lane_of(o), core)]
        to = device(lax.rem(x + dx, NX), yl, core, z, rho)
        return remote(piece, piece, x_s.at[dx - 1, e, o], x_r.at[dx - 1, e, o], to)

    def x_in(dx, e, o):
        far = lax.rem(x + NX - dx, NX)
        piece = cols.at[e, block(far, lane_of(o), core)]
        return remote(piece, piece, x_s.at[dx - 1, e, o], x_r.at[dx - 1, e, o], device(far, yl, core, z, rho))

    def s_copy(dx, e, o, side):
        piece = cols.at[e, block(lax.rem(x + NX - dx, NX), lane_of(o), side)]
        return remote(piece, piece, s_s.at[dx, e, o], s_r.at[dx, e, o], device(x, yl, 1 - core, z, rho))

    def spread(e, o):
        if o == 0:
            cols[e, blk] = rows[e, spin_rows(spin), :]
        for dx in (2, 1, 3):
            x_out(dx, e, o).start()
        s_copy(0, e, o, core).start()

    def relay(e, o):
        for dx in (1, 3, 2):
            x_in(dx, e, o).wait_recv()
            s_copy(dx, e, o, core).start()

    def whole(e):
        for dx in range(NX):
            for o in range(2):
                s_copy(dx, e, o, 1 - core).wait_recv()

    def prepare(e):
        for k in range(4):
            cos = wave[0, pl.ds(8 * k + e, 1), :]
            sin = wave[1, pl.ds(8 * k + e, 1), :]
            for s in range(4):
                for a in range(3):
                    ur = rows[e, pl.ds(16 * s, 16), pl.ds(a * 128, 128)].astype(F32)
                    ui = rows[e, pl.ds(16 * s, 16), pl.ds((3 + a) * 128, 128)].astype(F32)
                    re = ur * cos - ui * sin
                    im = ui * cos + ur * sin
                    re_hi, im_hi = re.astype(BF16), im.astype(BF16)
                    re_lo = (re - re_hi.astype(F32)).astype(BF16)
                    im_lo = (im - im_hi.astype(F32)).astype(BF16)
                    at = k * 128 + s * 32
                    for left, first, second in ((left_hi, re_hi, im_hi), (left_lo, re_lo, im_lo)):
                        left[e, pl.ds(at, 16), pl.ds(a * 128, 128)] = first
                        left[e, pl.ds(at, 16), pl.ds((3 + a) * 128, 128)] = second
                        left[e, pl.ds(at + 16, 16), pl.ds(a * 128, 128)] = -second
                        left[e, pl.ds(at + 16, 16), pl.ds((3 + a) * 128, 128)] = first

    def multiply(e, first=False, last=False):
        right = cols[e].reshape(256, KEY)
        for k in range(4):
            at = pl.ds(128 * k, 128)
            part = lax.dot_general(left_hi[e, at, :], right, ROWS, preferred_element_type=F32)
            part += lax.dot_general(left_lo[e, at, :], right, ROWS, preferred_element_type=F32)
            if not first:
                part += acc[at, :]
            if last:
                for half in range(4):
                    zsend[2 * k + half // 2, half % 2] = part[32 * half:32 * half + 32].astype(BF16)
            else:
                acc[at, :] = part

    def tell(turn):
        for side, to in enumerate(along_z if turn < 3 else along_y):
            pl.semaphore_signal(hand.at[turn, side], inc=1, device_id=to, device_id_type=MESH)

    def hear(turn):
        for side in range(2):
            pl.semaphore_wait(hand.at[turn, side], 1)

    pl.semaphore_wait(barrier, len(partners))
    y_out(1).start()
    z_out(2).start()
    a_out(0).start()
    spread(0, 0)
    d_out().start()
    a_out(3).start()
    a_out(1).start()
    a_out(2).start()
    tell(0)
    y_out(3).start()
    z_out(0).start()
    y_out(0).start()
    z_out(1).start()
    y_out(2).start()
    z_out(3).start()

    get_mom.wait()
    row = lax.broadcasted_iota(jnp.int32, (8, 128), 0)
    lane = lax.broadcasted_iota(jnp.int32, (8, 128), 1)
    hi_row = rho + (row & 1) * (flip(rho) - rho)
    z_row = z + (lax.shift_right_logical(row, 1) & 1) * (flip(z) - z)
    flat = ((z_row * 4 + hi_row) * 128 + lane).astype(F32)
    plane = jnp.floor((flat + 0.5) * (1.0 / (LEXT * LEXT)))
    line = jnp.floor((flat + 0.5) * (1.0 / LEXT))
    coords = (flat - LEXT * line, line - LEXT * plane, plane)
    for k in range(4):
        turns = sum(mom[k, d].astype(F32) * coords[d] for d in range(3))
        turns = turns - LEXT * jnp.floor((turns + 0.5) * (1.0 / LEXT))
        angle = turns * (TWO_PI / LEXT)
        wave[0, pl.ds(8 * k, 8), :] = jnp.cos(angle)
        wave[1, pl.ds(8 * k, 8), :] = jnp.sin(angle)

    prepare(0)
    a_in(0).wait_recv()
    spread(0, 1)
    g_in(2, 0).wait_recv()
    spread(2, 0)
    g_in(1, 0).wait_recv()
    spread(1, 0)
    a_in(2).wait_recv()
    spread(2, 1)
    a_in(1).wait_recv()
    spread(1, 1)
    g_in(3, 0).wait_recv()
    spread(3, 0)
    a_in(3).wait_recv()
    spread(3, 1)
    f_out(0).start()
    hear(0)
    tell(1)
    for j in (1, 3):
        g_in(1, j).wait_recv()
        f_out(j).start()
    g_in(1, 2).wait_recv()
    relay(0, 0)
    relay(0, 1)
    hear(1)
    tell(2)
    prepare(1)
    relay(2, 0)
    relay(1, 0)
    for j in (1, 2, 3):
        g_in(2, j).wait_recv()
    prepare(2)
    hear(2)
    tell(3)
    relay(2, 1)
    relay(1, 1)
    whole(0)
    multiply(0, first=True)
    for j in (1, 2, 3):
        g_in(3, j).wait_recv()
    prepare(3)
    relay(3, 0)
    whole(2)
    multiply(2)
    relay(3, 1)
    whole(1)
    multiply(1)
    whole(3)
    multiply(3, last=True)
    hear(3)

    def o_out(dz, sp):
        to = lax.rem(z + dz, NZ)
        half = lax.div(rho, 2)
        target = device(x, yl, core, to, sp * 2 + 1 - lax.rem(rho, 2))
        return remote(zsend.at[to, sp], zrecv.at[dz, half], z_s.at[dz, sp], z_r.at[dz, half], target)

    def o_in(dz, half):
        source = device(x, yl, core, lax.rem(z + NZ - dz, NZ), half * 2 + 1 - lax.rem(rho, 2))
        piece = zrecv.at[dz, half]
        return remote(piece, piece, z_s.at[dz, half], z_r.at[dz, half], source)

    for dz in (4, 3, 5, 2, 6, 1, 7, 0):
        for sp in range(2):
            o_out(dz, sp).start()

    for e in range(NH):
        a_out(e).wait_send()
        for o in range(2):
            for dx in range(1, NX):
                x_out(dx, e, o).wait_send()
            for dx in range(NX):
                s_copy(dx, e, o, core).wait_send()
        y_out(e).wait_send()
        z_out(e).wait_send()
        if e != 2:
            f_out(e).wait_send()
    d_out().wait_send()

    totals = [None, None]
    for dz in (0, 1, 7, 2, 6, 3, 5, 4):
        for half in range(2):
            o_in(dz, half).wait_recv()
            piece = zrecv[dz, half].astype(F32)
            totals[dz % 2] = piece if totals[dz % 2] is None else totals[dz % 2] + piece
    for odd in range(2):
        first = lax.rem(z + odd, 2) * 2
        for c in range(2):
            out_ref[first + c] = totals[odd][16 * c:16 * c + 16]
    for dz in range(NZ):
        for sp in range(2):
            o_out(dz, sp).wait_send()


def shards(modes, momenta):
    dma = pltpu.SemaphoreType.DMA
    return pl.pallas_call(
        kernel,
        out_shape=jax.ShapeDtypeStruct((4, 16, 256), F32),
        in_specs=[
            pl.BlockSpec(memory_space=pl.ANY),
            pl.BlockSpec(memory_space=pl.ANY),
        ],
        out_specs=pl.BlockSpec(memory_space=pltpu.VMEM),
        scratch_shapes=[
            pltpu.VMEM((2, 1, 12, 16, 128), BF16),
            pltpu.SMEM((4, 3), jnp.int32),
            pltpu.VMEM((NH, 64, KEY), BF16),
            pltpu.VMEM((NH, 16, 16, KEY), BF16),
            pltpu.VMEM((NH, 512, KEY), BF16),
            pltpu.VMEM((NH, 512, KEY), BF16),
            pltpu.VMEM((512, 256), F32),
            pltpu.VMEM((2, 32, 128), F32),
            pltpu.VMEM((NZ, 2, 32, 256), BF16),
            pltpu.VMEM((NZ, 2, 32, 256), BF16),
            pltpu.SemaphoreType.REGULAR((4, 2)),
            dma((2,)),
            dma((4, 4)), dma((3, 4)),
            dma((NH,)), dma((NH,)),
            dma((NX - 1, NH, 2)), dma((NX - 1, NH, 2)),
            dma((NX, NH, 2)), dma((NX, NH, 2)),
            dma((NZ, 2)), dma((NZ, 2)),
        ],
        compiler_params=pltpu.CompilerParams(
            collective_id=0, has_side_effects=True, vmem_limit_bytes=56 * 1024 * 1024
        ),
    )(jnp.transpose(modes, (0, 1, 3, 2, 4)), momenta)


def solution(mesh):
    placed = (P(None, None, "blk", None, "site"), P())
    return jax.shard_map(
        shards, mesh=mesh, in_specs=placed, out_specs=P("site", "blk", None), check_vma=False
    )
```

time: 46.9 us -> 43.7 us (0.932)
  the two profiles are of different devices: /device:TPU:4 before, /device:TPU:1 now
where the time goes in v3:
time: 43.7 us; the launch traced here: 43.5 us
  Pallas kernels  42.1 us (96%)
  local copies, waits for them, and re-layouts  1.47 us (3%)
    pallas_call x1, Pallas kernels, shards(): pl.pallas_call(kernel, out_shape=jax.ShapeDtypeStruct((4, 16, 256), F32),...  42.1 us
    unnamed x1, local copies, waits for them, and re-layouts  1.47 us

profile of v3, /device:TPU:1, one launch (start us, length us, event | category | flops | bytes accessed | tf_op | source)
XLA Modules:
  0.0 43.5 jit_solution(7142462376902822782)
XLA Ops:
  0.0 42.1 %shard_map.28 = f32[4,16,256]{2,1,0:T(8,128)} custom-call(bf16[2,1,12,16,128]{4,3,2,1,0:T(8,128)(2,1)} %bitcast.1, s32[4,3]{1,0:T(4,128)} %mom_ref.1), custom_call_target="tpu_custom_call" | custom-call | tf_op jit(solution)/shard_map/pallas_call | solution.py:321
  42.1 1.5 %copy.4 = f32[4,16,256]{2,1,0:T(8,128)} copy(f32[4,16,256]{2,1,0:T(8,128)} %shard_map.28) | data formatting | bytes 131072

commit v4 on v3

v4 whole, which is shorter than its diff:
```python
import math

import jax
import jax.numpy as jnp
from jax import lax
from jax.experimental import pallas as pl
from jax.experimental.pallas import tpu as pltpu
from jax.sharding import PartitionSpec as P

LEXT = 48
TWO_PI = 2.0 * math.pi
MESH = pl.DeviceIdType.MESH
F32 = jnp.float32
BF16 = jnp.bfloat16

NX, NZ, NH = 4, 8, 4
FAR = (0, 1, 3, 2)
SLOT = tuple(FAR.index(far) for far in range(NX))
KEY = 768
ROWS = (((1,), (1,)), ((), ()))


def remote(src, dst, send_sem, recv_sem, target):
    return pltpu.make_async_remote_copy(
        src_ref=src, dst_ref=dst, send_sem=send_sem, recv_sem=recv_sem,
        device_id=target, device_id_type=MESH,
    )


def flip(place):
    return place + 1 - 2 * lax.rem(place, 2)


def spin_rows(spin):
    return pl.ds(pl.multiple_of(spin * 16, 16), 16)


def kernel(
    modes_ref, mom_ref, out_ref,
    stage, mom, rows, cols, left, acc, acc_far, wave, near_out, near_in, far_out, far_in, tiles,
    hand, in_s, g_s, g_r, a_s, a_r, x_s, x_r, w_s, w_r, s_s, s_r, o_s, o_r,
):
    blk = lax.axis_index("blk")
    site = lax.axis_index("site")
    x = lax.div(blk, 4)
    yl = lax.rem(lax.div(blk, 2), 2)
    core = lax.rem(blk, 2)
    z = lax.div(site, 4)
    rho = lax.rem(site, 4)

    ahead = lax.rem(rho + 1 + 2 * yl, NH)
    behind = lax.rem(rho + 3 - 2 * yl, NH)

    def z_of(e):
        return flip(z) if e // 2 else z

    def spin_of(e):
        hi = lax.rem(rho + e, 2)
        return (1 - hi) * 2 + lax.rem(z_of(e), 2)

    spin = spin_of(0)

    def device(x, yl, core, z, hi):
        return (x * 4 + yl * 2 + core, z * 4 + hi)

    def lane_of(o):
        return yl if o == 0 else 1 - yl

    barrier = pltpu.get_barrier_semaphore()
    partners = [device(x, yl, 1 - core, z, rho)]
    partners += [device(lax.rem(x + dx, NX), yl, core, z, rho) for dx in (1, NX - 1)]
    partners += [device(x, 1 - yl, core, z_of(e), ahead if e % 2 else rho) for e in range(NH)]
    partners += [device(x, yl, core, flip(z), hi) for hi in (ahead, behind)]
    along_z = [device(x, yl, core, lax.rem(z + dz, NZ), rho) for dz in (2, NZ - 2, 1, NZ - 1)]
    along_y = [device(x, yl, core, z, lax.rem(rho + dh, NH)) for dh in (1, NH - 1)]
    partners += along_z + along_y
    for target in partners:
        pl.semaphore_signal(barrier, inc=1, device_id=target, device_id_type=MESH)
    get_modes = pltpu.make_async_copy(modes_ref, stage, in_s.at[0])
    get_modes.start()
    get_mom = pltpu.make_async_copy(mom_ref, mom, in_s.at[1])
    get_mom.start()

    get_modes.wait()
    for c in range(2):
        for s in range(4):
            for a in range(3):
                rows[0, pl.ds(16 * s, 16), pl.ds((c * 3 + a) * 128, 128)] = stage[c, 0, 3 * s + a]

    def gather(e, spin_e, e_from, to, way=0):
        return remote(
            rows.at[e_from, spin_rows(spin_e), :], rows.at[e, spin_rows(spin_e), :],
            g_s.at[e - 1 + way, spin_e], g_r.at[e - 1, spin_e], to,
        )

    def y_out(j):
        return gather(1, spin_of(j), 0, device(x, yl, core, z, behind))

    def z_out(j):
        return gather(2, spin_of(j), 0, device(x, yl, core, flip(z), rho))

    def d_out():
        return gather(3, spin_of(3), 0, device(x, yl, core, flip(z), behind), 1)

    def f_out(j):
        return gather(3, spin_of(j), 1, device(x, yl, core, flip(z), rho))

    def g_in(e, j):
        to = device(x, yl, core, flip(z), rho) if e > 1 else device(x, yl, core, z, ahead)
        return gather(e, spin_of(j), e, to)

    def piece(e, far, o, side):
        return cols.at[e, SLOT[far % NX], 0, lane_of(o), side]

    def a_out(e):
        to = device(x, 1 - yl, core, z_of(e), ahead if e % 2 else rho)
        return remote(rows.at[0, spin_rows(spin_of(e)), :], piece(e, 0, 0, core), a_s.at[e], a_r.at[e], to)

    def a_in(e):
        into = piece(e, 0, 1, core)
        return remote(into, into, a_s.at[e], a_r.at[e], device(x, 1 - yl, core, z_of(e), ahead if e % 2 else rho))

    def along_x(dx):
        return device(lax.rem(x + dx + NX, NX), yl, core, z, rho)

    def x_out(dx, e, o):
        at = (dx + 1) // 2
        return remote(
            piece(e, 0, o, core), piece(e, -dx, o, core), x_s.at[at, e, o], x_r.at[at, e, o], along_x(dx)
        )

    def x_in(dx, e, o):
        at, into = (dx + 1) // 2, piece(e, -dx, o, core)
        return remote(into, into, x_s.at[at, e, o], x_r.at[at, e, o], along_x(dx))

    def w_out(e, o):
        dx = 1 - 2 * o
        return remote(piece(e, -dx, o, core), piece(e, 2, o, core), w_s.at[e, o], w_r.at[e, o], along_x(dx))

    def w_in(e, o):
        into = piece(e, 2, o, core)
        return remote(into, into, w_s.at[e, o], w_r.at[e, o], along_x(1 - 2 * o))

    def s_copy(far, e, o, side):
        at = SLOT[far % NX]
        both = piece(e, far, o, side)
        return remote(both, both, s_s.at[at, e, o], s_r.at[at, e, o], device(x, yl, 1 - core, z, rho))

    def spread(e, o):
        if o == 0:
            cols[e, 0, 0, yl, core] = rows[e, spin_rows(spin), :]
        x_out(1, e, o).start()
        x_out(-1, e, o).start()
        s_copy(0, e, o, core).start()

    def relay(e, o):
        x_in(1, e, o).wait_recv()
        x_in(-1, e, o).wait_recv()
        w_out(e, o).start()
        s_copy(1, e, o, core).start()
        s_copy(-1, e, o, core).start()

    def relay_far(e, o):
        w_in(e, o).wait_recv()
        s_copy(2, e, o, core).start()

    def whole(e, far):
        for o in range(2):
            s_copy(far, e, o, 1 - core).wait_recv()
        at = SLOT[far % NX]
        for l in range(2):
            for side in range(2):
                for a in range(3):
                    cols[e, at, 1, l, side, :, pl.ds(a * 128, 128)] = cols[e, at, 0, l, side, :, pl.ds((3 + a) * 128, 128)]
                    cols[e, at, 1, l, side, :, pl.ds((3 + a) * 128, 128)] = -cols[e, at, 0, l, side, :, pl.ds(a * 128, 128)]

    def prepare(e):
        for k in range(4):
            cos = wave[0, pl.ds(8 * k + e, 1), :]
            sin = wave[1, pl.ds(8 * k + e, 1), :]
            for s in range(4):
                for a in range(3):
                    ur = rows[e, pl.ds(16 * s, 16), pl.ds(a * 128, 128)].astype(F32)
                    ui = rows[e, pl.ds(16 * s, 16), pl.ds((3 + a) * 128, 128)].astype(F32)
                    for c, value in enumerate((ur * cos - ui * sin, ui * cos + ur * sin)):
                        high = value.astype(BF16)
                        at, lanes = k * 64 + s * 16, pl.ds((3 * c + a) * 128, 128)
                        left[e, pl.ds(at, 16), lanes] = high
                        left[e, pl.ds(256 + at, 16), lanes] = (value - high.astype(F32)).astype(BF16)

    def product(e, right):
        part = lax.dot_general(left[e], right, ROWS, preferred_element_type=F32)
        return part[:256] + part[256:]

    def put(out, sums, slots):
        for k in range(4):
            for s in range(4):
                for slot in range(slots):
                    tile = sums[64 * k + 16 * s:64 * k + 16 * s + 16, 128 * slot:128 * slot + 128]
                    out[2 * k + s // 2, s % 2, slot] = tile.astype(BF16)

    def multiply_near(e, first=False, last=False):
        part = product(e, cols[e, pl.ds(0, 3)].reshape(384, KEY))
        if not first:
            part += acc[...]
        if last:
            put(near_out, part, 3)
        else:
            acc[...] = part

    def multiply_far(es, first=False, last=False):
        part = None if first else acc_far[...]
        for e in es:
            more = product(e, cols[e, 3].reshape(128, KEY))
            part = more if part is None else part + more
        if last:
            put(far_out, part, 1)
        else:
            acc_far[...] = part

    def tell(turn):
        for side, to in enumerate(along_y if turn else along_z[:2]):
            pl.semaphore_signal(hand.at[turn, side], inc=1, device_id=to, device_id_type=MESH)

    def hear(turn):
        for side in range(2):
            pl.semaphore_wait(hand.at[turn, side], 1)

    def o_out(part, dz, sp):
        to = lax.rem(z + dz, NZ)
        half = lax.div(rho, 2)
        target = device(x, yl, core, to, sp * 2 + 1 - lax.rem(rho, 2))
        src, dst = ((near_out, near_in), (far_out, far_in))[part]
        return remote(src.at[to, sp], dst.at[dz, half], o_s.at[part, dz, sp], o_r.at[part, dz, half], target)

    def o_in(part, dz, half):
        source = device(x, yl, core, lax.rem(z + NZ - dz, NZ), half * 2 + 1 - lax.rem(rho, 2))
        into = (near_in, far_in)[part].at[dz, half]
        return remote(into, into, o_s.at[part, dz, half], o_r.at[part, dz, half], source)

    def scatter(part):
        for dz in (4, 3, 5, 2, 6, 1, 7, 0):
            for sp in range(2):
                o_out(part, dz, sp).start()

    pl.semaphore_wait(barrier, len(partners))
    y_out(1).start()
    z_out(2).start()
    a_out(0).start()
    spread(0, 0)
    d_out().start()
    a_out(3).start()
    a_out(1).start()
    a_out(2).start()
    tell(0)

    get_mom.wait()
    row = lax.broadcasted_iota(jnp.int32, (8, 128), 0)
    lane = lax.broadcasted_iota(jnp.int32, (8, 128), 1)
    hi_row = rho + (row & 1) * (ahead - rho)
    z_row = z + (lax.shift_right_logical(row, 1) & 1) * (flip(z) - z)
    flat = ((z_row * 4 + hi_row) * 128 + lane).astype(F32)
    plane = jnp.floor((flat + 0.5) * (1.0 / (LEXT * LEXT)))
    line = jnp.floor((flat + 0.5) * (1.0 / LEXT))
    coords = (flat - LEXT * line, line - LEXT * plane, plane)
    for k in range(4):
        turns = sum(mom[k, d].astype(F32) * coords[d] for d in range(3))
        turns = turns - LEXT * jnp.floor((turns + 0.5) * (1.0 / LEXT))
        angle = turns * (TWO_PI / LEXT)
        wave[0, pl.ds(8 * k, 8), :] = jnp.cos(angle)
        wave[1, pl.ds(8 * k, 8), :] = jnp.sin(angle)

    prepare(0)
    a_in(0).wait_recv()
    spread(0, 1)
    g_in(2, 0).wait_recv()
    spread(2, 0)
    g_in(1, 0).wait_recv()
    spread(1, 0)
    f_out(0).start()
    y_out(0).start()
    z_out(0).start()
    y_out(2).start()
    z_out(1).start()
    y_out(3).start()
    z_out(3).start()
    a_in(2).wait_recv()
    spread(2, 1)
    relay(0, 0)
    a_in(1).wait_recv()
    spread(1, 1)
    g_in(3, 0).wait_recv()
    spread(3, 0)
    a_in(3).wait_recv()
    spread(3, 1)
    relay(0, 1)
    relay(2, 0)
    g_in(1, 1).wait_recv()
    f_out(1).start()
    relay(1, 0)
    relay(2, 1)
    g_in(1, 3).wait_recv()
    f_out(3).start()
    hear(0)
    tell(1)
    relay(1, 1)
    relay(3, 0)
    relay(3, 1)
    for j in (1, 2, 3):
        g_in(2, j).wait_recv()
    prepare(2)
    relay_far(0, 0)
    relay_far(0, 1)
    g_in(1, 2).wait_recv()
    prepare(1)
    for far in (0, 1, -1):
        whole(0, far)
    multiply_near(0, first=True)
    relay_far(2, 0)
    relay_far(1, 0)
    for far in (0, 1, -1):
        whole(2, far)
    multiply_near(2)
    relay_far(2, 1)
    relay_far(1, 1)
    for far in (0, 1, -1):
        whole(1, far)
    multiply_near(1)
    for j in (1, 2, 3):
        g_in(3, j).wait_recv()
    prepare(3)
    relay_far(3, 0)
    relay_far(3, 1)
    for far in (0, 1, -1):
        whole(3, far)
    multiply_near(3, last=True)
    hear(1)
    scatter(0)
    for e in (0, 2, 1):
        whole(e, 2)
    multiply_far((0, 2, 1), first=True)
    whole(3, 2)
    multiply_far((3,), last=True)
    scatter(1)

    for e in range(NH):
        a_out(e).wait_send()
        for o in range(2):
            x_out(1, e, o).wait_send()
            x_out(-1, e, o).wait_send()
            w_out(e, o).wait_send()
            for far in range(NX):
                s_copy(far, e, o, core).wait_send()
        y_out(e).wait_send()
        z_out(e).wait_send()
        if e != 2:
            f_out(e).wait_send()
    d_out().wait_send()

    for part, slots in ((0, 3), (1, 1)):
        totals = [None, None]
        for dz in (0, 1, 7, 2, 6, 3, 5, 4):
            for half in range(2):
                o_in(part, dz, half).wait_recv()
                some = (near_in, far_in)[part][dz, half].astype(F32)
                totals[dz % 2] = some if totals[dz % 2] is None else totals[dz % 2] + some
        for odd in range(2):
            for slot in range(slots):
                far = FAR[3 * part + slot]
                tiles[lax.rem(z + odd, 2), lax.rem(x + far, NX)] = totals[odd][slot]
    low = lax.broadcasted_iota(jnp.int32, (16, 128), 1) < 64
    for r in range(2):
        for v in range(2):
            even, odd = tiles[r, 2 * v], tiles[r, 2 * v + 1]
            out_ref[2 * r, :, pl.ds(128 * v, 128)] = jnp.where(low, even, pltpu.roll(odd, 64, 1))
            out_ref[2 * r + 1, :, pl.ds(128 * v, 128)] = jnp.where(low, pltpu.roll(even, 64, 1), odd)
    for part in range(2):
        for dz in range(NZ):
            for sp in range(2):
                o_out(part, dz, sp).wait_send()


def shards(modes, momenta):
    dma = pltpu.SemaphoreType.DMA
    return pl.pallas_call(
        kernel,
        out_shape=jax.ShapeDtypeStruct((4, 16, 256), F32),
        in_specs=[
            pl.BlockSpec(memory_space=pl.ANY),
            pl.BlockSpec(memory_space=pl.ANY),
        ],
        out_specs=pl.BlockSpec(memory_space=pltpu.VMEM),
        scratch_shapes=[
            pltpu.VMEM((2, 1, 12, 16, 128), BF16),
            pltpu.SMEM((4, 3), jnp.int32),
            pltpu.VMEM((NH, 64, KEY), BF16),
            pltpu.VMEM((NH, NX, 2, 2, 2, 16, KEY), BF16),
            pltpu.VMEM((NH, 512, KEY), BF16),
            pltpu.VMEM((256, 384), F32),
            pltpu.VMEM((256, 128), F32),
            pltpu.VMEM((2, 32, 128), F32),
            pltpu.VMEM((NZ, 2, 3, 16, 128), BF16),
            pltpu.VMEM((NZ, 2, 3, 16, 128), BF16),
            pltpu.VMEM((NZ, 2, 1, 16, 128), BF16),
            pltpu.VMEM((NZ, 2, 1, 16, 128), BF16),
            pltpu.VMEM((2, NX, 16, 128), F32),
            pltpu.SemaphoreType.REGULAR((2, 2)),
            dma((2,)),
            dma((4, 4)), dma((3, 4)),
            dma((NH,)), dma((NH,)),
            dma((2, NH, 2)), dma((2, NH, 2)),
            dma((NH, 2)), dma((NH, 2)),
            dma((NX, NH, 2)), dma((NX, NH, 2)),
            dma((2, NZ, 2)), dma((2, NZ, 2)),
        ],
        compiler_params=pltpu.CompilerParams(
            collective_id=0, has_side_effects=True, vmem_limit_bytes=56 * 1024 * 1024
        ),
    )(jnp.transpose(modes, (0, 1, 3, 2, 4)), momenta)


def solution(mesh):
    placed = (P(None, None, "blk", None, "site"), P())
    return jax.shard_map(
        shards, mesh=mesh, in_specs=placed, out_specs=P("site", "blk", None), check_vma=False
    )
```

time: 43.7 us -> 42.3 us (0.968)
  Pallas kernels: 42.1 us -> 40.4 us
    pallas_call x1, Pallas kernels: 42.1 us -> 40.4 us  [shards(): pl.pallas_call(kernel, out_shape=jax.ShapeDtypeStruct((4, 16, 256), F32),...]
where the time goes in v4:
time: 42.3 us; the launch traced here: 41.9 us
  Pallas kernels  40.4 us (96%)
  local copies, waits for them, and re-layouts  1.47 us (3%)
    pallas_call x1, Pallas kernels, shards(): pl.pallas_call(kernel, out_shape=jax.ShapeDtypeStruct((4, 16, 256), F32),...  40.4 us
    unnamed x1, local copies, waits for them, and re-layouts  1.47 us

profile of v4, /device:TPU:1, one launch (start us, length us, event | category | flops | bytes accessed | tf_op | source)
XLA Modules:
  0.0 41.9 jit_solution(3797287458326988644)
XLA Ops:
  0.0 40.4 %shard_map.28 = f32[4,16,256]{2,1,0:T(8,128)} custom-call(bf16[2,1,12,16,128]{4,3,2,1,0:T(8,128)(2,1)} %bitcast.1, s32[4,3]{1,0:T(4,128)} %mom_ref.1), custom_call_target="tpu_custom_call" | custom-call | tf_op jit(solution)/shard_map/pallas_call | solution.py:385
  40.4 1.5 %copy.4 = f32[4,16,256]{2,1,0:T(8,128)} copy(f32[4,16,256]{2,1,0:T(8,128)} %shard_map.28) | data formatting | bytes 131072

commit v5 on v4

--- a/solution.py
+++ b/solution.py
@@ -48,8 +48,8 @@
     z = lax.div(site, 4)
     rho = lax.rem(site, 4)
 
-    ahead = lax.rem(rho + 1 + 2 * yl, NH)
-    behind = lax.rem(rho + 3 - 2 * yl, NH)
+    ahead = lax.rem(rho + 3 + 2 * yl, NH)
+    behind = lax.rem(rho + 1 + 2 * yl, NH)
 
     def z_of(e):
         return flip(z) if e // 2 else z
@@ -87,10 +87,10 @@
             for a in range(3):
                 rows[0, pl.ds(16 * s, 16), pl.ds((c * 3 + a) * 128, 128)] = stage[c, 0, 3 * s + a]
 
-    def gather(e, spin_e, e_from, to, way=0):
+    def gather(e, spin_e, e_from, to):
         return remote(
             rows.at[e_from, spin_rows(spin_e), :], rows.at[e, spin_rows(spin_e), :],
-            g_s.at[e - 1 + way, spin_e], g_r.at[e - 1, spin_e], to,
+            g_s.at[e - 1, spin_e], g_r.at[e - 1, spin_e], to,
         )
 
     def y_out(j):
@@ -99,11 +99,8 @@
     def z_out(j):
         return gather(2, spin_of(j), 0, device(x, yl, core, flip(z), rho))
 
-    def d_out():
-        return gather(3, spin_of(3), 0, device(x, yl, core, flip(z), behind), 1)
-
-    def f_out(j):
-        return gather(3, spin_of(j), 1, device(x, yl, core, flip(z), rho))
+    def d_out(j):
+        return gather(3, spin_of(j), 0, device(x, yl, core, flip(z), behind))
 
     def g_in(e, j):
         to = device(x, yl, core, flip(z), rho) if e > 1 else device(x, yl, core, z, ahead)
@@ -141,32 +138,27 @@
         into = piece(e, 2, o, core)
         return remote(into, into, w_s.at[e, o], w_r.at[e, o], along_x(1 - 2 * o))
 
-    def s_copy(far, e, o, side):
+    def s_copy(far, e, side):
         at = SLOT[far % NX]
-        both = piece(e, far, o, side)
-        return remote(both, both, s_s.at[at, e, o], s_r.at[at, e, o], device(x, yl, 1 - core, z, rho))
+        both = cols.at[e, at, 0, :, side]
+        return remote(both, both, s_s.at[at, e], s_r.at[at, e], device(x, yl, 1 - core, z, rho))
 
     def spread(e, o):
         if o == 0:
             cols[e, 0, 0, yl, core] = rows[e, spin_rows(spin), :]
         x_out(1, e, o).start()
         x_out(-1, e, o).start()
-        s_copy(0, e, o, core).start()
 
     def relay(e, o):
         x_in(1, e, o).wait_recv()
         x_in(-1, e, o).wait_recv()
         w_out(e, o).start()
-        s_copy(1, e, o, core).start()
-        s_copy(-1, e, o, core).start()
 
     def relay_far(e, o):
         w_in(e, o).wait_recv()
-        s_copy(2, e, o, core).start()
 
     def whole(e, far):
-        for o in range(2):
-            s_copy(far, e, o, 1 - core).wait_recv()
+        s_copy(far, e, 1 - core).wait_recv()
         at = SLOT[far % NX]
         for l in range(2):
             for side in range(2):
@@ -248,7 +240,7 @@
     z_out(2).start()
     a_out(0).start()
     spread(0, 0)
-    d_out().start()
+    d_out(3).start()
     a_out(3).start()
     a_out(1).start()
     a_out(2).start()
@@ -270,6 +262,10 @@
         wave[0, pl.ds(8 * k, 8), :] = jnp.cos(angle)
         wave[1, pl.ds(8 * k, 8), :] = jnp.sin(angle)
 
+    def share(e):
+        for far in (1, -1):
+            s_copy(far, e, core).start()
+
     prepare(0)
     a_in(0).wait_recv()
     spread(0, 1)
@@ -277,13 +273,11 @@
     spread(2, 0)
     g_in(1, 0).wait_recv()
     spread(1, 0)
-    f_out(0).start()
-    y_out(0).start()
-    z_out(0).start()
-    y_out(2).start()
-    z_out(1).start()
-    y_out(3).start()
-    z_out(3).start()
+    for j, i in ((0, 0), (2, 1), (3, 3)):
+        z_out(i).start()
+        y_out(j).start()
+        d_out(j if j < 3 else 1).start()
+    s_copy(0, 0, core).start()
     a_in(2).wait_recv()
     spread(2, 1)
     relay(0, 0)
@@ -293,44 +287,48 @@
     spread(3, 0)
     a_in(3).wait_recv()
     spread(3, 1)
+    for e in (2, 1, 3):
+        s_copy(0, e, core).start()
     relay(0, 1)
+    share(0)
     relay(2, 0)
-    g_in(1, 1).wait_recv()
-    f_out(1).start()
     relay(1, 0)
     relay(2, 1)
-    g_in(1, 3).wait_recv()
-    f_out(3).start()
+    share(2)
     hear(0)
     tell(1)
     relay(1, 1)
+    share(1)
     relay(3, 0)
     relay(3, 1)
+    share(3)
+    def far_of(e):
+        relay_far(e, 0)
+        relay_far(e, 1)
+        s_copy(2, e, core).start()
+
     for j in (1, 2, 3):
         g_in(2, j).wait_recv()
     prepare(2)
-    relay_far(0, 0)
-    relay_far(0, 1)
-    g_in(1, 2).wait_recv()
-    prepare(1)
+    far_of(0)
     for far in (0, 1, -1):
         whole(0, far)
     multiply_near(0, first=True)
-    relay_far(2, 0)
-    relay_far(1, 0)
+    for j in (1, 2, 3):
+        g_in(1, j).wait_recv()
+    prepare(1)
+    far_of(2)
     for far in (0, 1, -1):
         whole(2, far)
     multiply_near(2)
-    relay_far(2, 1)
-    relay_far(1, 1)
+    far_of(1)
     for far in (0, 1, -1):
         whole(1, far)
     multiply_near(1)
     for j in (1, 2, 3):
         g_in(3, j).wait_recv()
     prepare(3)
-    relay_far(3, 0)
-    relay_far(3, 1)
+    far_of(3)
     for far in (0, 1, -1):
         whole(3, far)
     multiply_near(3, last=True)
@@ -349,13 +347,16 @@
             x_out(1, e, o).wait_send()
             x_out(-1, e, o).wait_send()
             w_out(e, o).wait_send()
-            for far in range(NX):
-                s_copy(far, e, o, core).wait_send()
+        for far in range(NX):
+            s_copy(far, e, core).wait_send()
         y_out(e).wait_send()
         z_out(e).wait_send()
-        if e != 2:
-            f_out(e).wait_send()
-    d_out().wait_send()
+        d_out(e).wait_send()
+
+    for part in range(2):
+        for dz in range(NZ):
+            for sp in range(2):
+                o_out(part, dz, sp).wait_send()
 
     for part, slots in ((0, 3), (1, 1)):
         totals = [None, None]
@@ -374,10 +375,6 @@
             even, odd = tiles[r, 2 * v], tiles[r, 2 * v + 1]
             out_ref[2 * r, :, pl.ds(128 * v, 128)] = jnp.where(low, even, pltpu.roll(odd, 64, 1))
             out_ref[2 * r + 1, :, pl.ds(128 * v, 128)] = jnp.where(low, pltpu.roll(even, 64, 1), odd)
-    for part in range(2):
-        for dz in range(NZ):
-            for sp in range(2):
-                o_out(part, dz, sp).wait_send()
 
 
 def shards(modes, momenta):
@@ -406,11 +403,11 @@
             pltpu.VMEM((2, NX, 16, 128), F32),
             pltpu.SemaphoreType.REGULAR((2, 2)),
             dma((2,)),
-            dma((4, 4)), dma((3, 4)),
+            dma((3, 4)), dma((3, 4)),
             dma((NH,)), dma((NH,)),
             dma((2, NH, 2)), dma((2, NH, 2)),
             dma((NH, 2)), dma((NH, 2)),
-            dma((NX, NH, 2)), dma((NX, NH, 2)),
+            dma((NX, NH)), dma((NX, NH)),
             dma((2, NZ, 2)), dma((2, NZ, 2)),
         ],
         compiler_params=pltpu.CompilerParams(

time: 42.3 us -> 39.7 us (0.939)
  Pallas kernels: 40.4 us -> 38 us
    pallas_call x1, Pallas kernels: 40.4 us -> 38 us  [shards(): pl.pallas_call(kernel, out_shape=jax.ShapeDtypeStruct((4, 16, 256), F32),...]
where the time goes in v5:
time: 39.7 us; the launch traced here: 39.5 us
  Pallas kernels  38 us (96%)
  local copies, waits for them, and re-layouts  1.47 us (4%)
    pallas_call x1, Pallas kernels, shards(): pl.pallas_call(kernel, out_shape=jax.ShapeDtypeStruct((4, 16, 256), F32),...  38 us
    unnamed x1, local copies, waits for them, and re-layouts  1.47 us

profile of v5, /device:TPU:1, one launch (start us, length us, event | category | flops | bytes accessed | tf_op | source)
XLA Modules:
  0.0 39.5 jit_solution(3741738744039353044)
XLA Ops:
  0.0 38.0 %shard_map.28 = f32[4,16,256]{2,1,0:T(8,128)} custom-call(bf16[2,1,12,16,128]{4,3,2,1,0:T(8,128)(2,1)} %bitcast.1, s32[4,3]{1,0:T(4,128)} %mom_ref.1), custom_call_target="tpu_custom_call" | custom-call | tf_op jit(solution)/shard_map/pallas_call | solution.py:382
  38.0 1.5 %copy.4 = f32[4,16,256]{2,1,0:T(8,128)} copy(f32[4,16,256]{2,1,0:T(8,128)} %shard_map.28) | data formatting | bytes 131072

commit v6 on v5

--- a/solution.py
+++ b/solution.py
@@ -265,6 +265,11 @@
     def share(e):
         for far in (1, -1):
             s_copy(far, e, core).start()
+
+    def far_of(e):
+        relay_far(e, 0)
+        relay_far(e, 1)
+        s_copy(2, e, core).start()
 
     prepare(0)
     a_in(0).wait_recv()
@@ -297,43 +302,38 @@
     share(2)
     hear(0)
     tell(1)
+    for j in (1, 2, 3):
+        g_in(2, j).wait_recv()
+    prepare(2)
     relay(1, 1)
     share(1)
+    for far in (0, 1, -1):
+        whole(0, far)
+    multiply_near(0, first=True)
     relay(3, 0)
     relay(3, 1)
     share(3)
-    def far_of(e):
-        relay_far(e, 0)
-        relay_far(e, 1)
-        s_copy(2, e, core).start()
-
-    for j in (1, 2, 3):
-        g_in(2, j).wait_recv()
-    prepare(2)
-    far_of(0)
-    for far in (0, 1, -1):
-        whole(0, far)
-    multiply_near(0, first=True)
     for j in (1, 2, 3):
         g_in(1, j).wait_recv()
     prepare(1)
-    far_of(2)
+    far_of(0)
     for far in (0, 1, -1):
         whole(2, far)
     multiply_near(2)
+    far_of(2)
+    for j in (1, 2, 3):
+        g_in(3, j).wait_recv()
+    prepare(3)
     far_of(1)
     for far in (0, 1, -1):
         whole(1, far)
     multiply_near(1)
-    for j in (1, 2, 3):
-        g_in(3, j).wait_recv()
-    prepare(3)
-    far_of(3)
     for far in (0, 1, -1):
         whole(3, far)
     multiply_near(3, last=True)
     hear(1)
     scatter(0)
+    far_of(3)
     for e in (0, 2, 1):
         whole(e, 2)
     multiply_far((0, 2, 1), first=True)

time: 39.7 us -> 39.4 us (level)
  no operation moved by 1% of the time
where the time goes in v6:
time: 39.4 us; the launch traced here: 39.2 us
  Pallas kernels  37.8 us (96%)
  local copies, waits for them, and re-layouts  1.47 us (4%)
    pallas_call x1, Pallas kernels, shards(): pl.pallas_call(kernel, out_shape=jax.ShapeDtypeStruct((4, 16, 256), F32),...  37.8 us
    unnamed x1, local copies, waits for them, and re-layouts  1.47 us

profile of v6, /device:TPU:1, one launch (start us, length us, event | category | flops | bytes accessed | tf_op | source)
XLA Modules:
  0.0 39.2 jit_solution(15360129088747392455)
XLA Ops:
  0.0 37.8 %shard_map.28 = f32[4,16,256]{2,1,0:T(8,128)} custom-call(bf16[2,1,12,16,128]{4,3,2,1,0:T(8,128)(2,1)} %bitcast.1, s32[4,3]{1,0:T(4,128)} %mom_ref.1), custom_call_target="tpu_custom_call" | custom-call | tf_op jit(solution)/shard_map/pallas_call | solution.py:382
  37.8 1.5 %copy.4 = f32[4,16,256]{2,1,0:T(8,128)} copy(f32[4,16,256]{2,1,0:T(8,128)} %shard_map.28) | data formatting | bytes 131072

commit v7 on v6

--- a/solution.py
+++ b/solution.py
@@ -234,17 +234,6 @@
         for dz in (4, 3, 5, 2, 6, 1, 7, 0):
             for sp in range(2):
                 o_out(part, dz, sp).start()
-
-    pl.semaphore_wait(barrier, len(partners))
-    y_out(1).start()
-    z_out(2).start()
-    a_out(0).start()
-    spread(0, 0)
-    d_out(3).start()
-    a_out(3).start()
-    a_out(1).start()
-    a_out(2).start()
-    tell(0)
 
     get_mom.wait()
     row = lax.broadcasted_iota(jnp.int32, (8, 128), 0)
@@ -265,6 +254,17 @@
     def share(e):
         for far in (1, -1):
             s_copy(far, e, core).start()
+
+    pl.semaphore_wait(barrier, len(partners))
+    y_out(1).start()
+    z_out(2).start()
+    a_out(0).start()
+    spread(0, 0)
+    d_out(3).start()
+    a_out(3).start()
+    a_out(1).start()
+    a_out(2).start()
+    tell(0)
 
     def far_of(e):
         relay_far(e, 0)

time: 39.4 us -> 39.4 us (level)
  no operation moved by 1% of the time
where the time goes in v7:
time: 39.4 us; the launch traced here: 39.2 us
  Pallas kernels  37.8 us (96%)
  local copies, waits for them, and re-layouts  1.47 us (4%)
    pallas_call x1, Pallas kernels, shards(): pl.pallas_call(kernel, out_shape=jax.ShapeDtypeStruct((4, 16, 256), F32),...  37.8 us
    unnamed x1, local copies, waits for them, and re-layouts  1.47 us

profile of v7, /device:TPU:1, one launch (start us, length us, event | category | flops | bytes accessed | tf_op | source)
XLA Modules:
  0.0 39.2 jit_solution(10666621927838265983)
XLA Ops:
  0.0 37.8 %shard_map.28 = f32[4,16,256]{2,1,0:T(8,128)} custom-call(bf16[2,1,12,16,128]{4,3,2,1,0:T(8,128)(2,1)} %bitcast.1, s32[4,3]{1,0:T(4,128)} %mom_ref.1), custom_call_target="tpu_custom_call" | custom-call | tf_op jit(solution)/shard_map/pallas_call | solution.py:382
  37.8 1.5 %copy.4 = f32[4,16,256]{2,1,0:T(8,128)} copy(f32[4,16,256]{2,1,0:T(8,128)} %shard_map.28) | data formatting | bytes 131072
